TPU v7x, 512 devices: a whole 4x4x16 slice. The times are simulated.
512 devices in a mesh: freq: 16 (over x, y_lo, core), vis: 32 (over z, y_hi).
Axes of the slice: x: 4, y: 4 (y_hi: 2, y_lo: 2; y = y_hi * 2 + y_lo), z: 16, core: 2. Of those that a mesh axis runs over, the one named last changes fastest.
Arguments:
- model: bfloat16 [256, 4096], P('vis'), may hold values from -0.01171875 to 0.01171875
- beam: bfloat16 [16, 256, 1024], P('freq', 'vis'), may hold values from 0.25 to 1.75
- vis_obs: float32 [16, 32, 2, 2048], P('freq', 'vis'), may hold values from -6 to 6
- vis_uv: float32 [16, 32, 2, 2048], P('freq', 'vis'), may hold values from 0 to 64
- spectral: float32 [16, 32, 2048], P('freq', 'vis'), may hold values from -1 to 1
- vis_subgrid: int32 [16, 32, 2048], P('freq', 'vis'), may hold values from 0 to 1
- counts: int32 [16, 32], P('freq', 'vis'), may hold values from 512 to 2048, as said below
- uv_offsets: int32 [16, 32, 2, 2], P('freq', 'vis'), may hold values from -128 to 127
- w_planes: int32 [16, 32, 2], P('freq', 'vis'), may hold values from 0 to 31
Outputs:
- residual_vis: float32 [16, 32, 2, 2048], P('freq', 'vis')
- dirty: float32 [256, 4096], P('vis')
Inputs may be any that keep to these rules, and one draw needn't show every extreme that they name: `counts`: each block has at least 512 live visibilities; some block is full.
All inputs are finite; a program needn't handle non-finite values.
Results may differ from a plain program's by a relative error of at most 0.008.
Values may be sent and summed in bfloat16 or wider, within the bound.
A program may use at most 64 MiB of HBM per device.

v0:
```python
import math

import jax
import jax.numpy as jnp
from jax import lax
from jax.sharding import PartitionSpec as P

S = 64


KERNEL_WIDTH = 0.5


def axis_table(cell_index, pixels, w_plane, modulus):
    linear = jnp.mod(cell_index[:, None] * pixels[None, :], modulus)
    wrap_mod = 2 * modulus * modulus
    quadratic = jnp.mod(w_plane * pixels * pixels, wrap_mod)
    fraction = (
        linear.astype(jnp.float32) / modulus + (quadratic.astype(jnp.float32) / wrap_mod)[None, :]
    )
    phases = -2.0 * math.pi * fraction
    return (jnp.cos(phases).astype(jnp.bfloat16), jnp.sin(phases).astype(jnp.bfloat16))


def kernel_table(position, members, cell_count):
    cell_pos = jnp.arange(cell_count, dtype=jnp.float32)
    offset_cells = position[None, :] - cell_pos[:, None]
    values = jnp.exp(offset_cells * offset_cells * (-0.5 / (KERNEL_WIDTH * KERNEL_WIDTH)))
    return (values * members[None, :]).astype(jnp.bfloat16)


def shards(model, beam, vis_obs, vis_uv, spectral, vis_subgrid, counts, uv_offsets, w_planes):
    rows_own = model.shape[0]
    facet_side = beam.shape[-1]
    taylor_count = model.shape[1] // facet_side
    block_count = lax.axis_size("vis")
    extent = rows_own * block_count
    sub_count = w_planes.shape[-1]
    vis_count = vis_obs.shape[-1]
    norm_scale = 1.0 / (S * math.sqrt(lax.axis_size("freq") * block_count * sub_count))
    cell_index = jnp.arange(S, dtype=jnp.int32) - S // 2
    m_pixels = jnp.arange(facet_side, dtype=jnp.int32) - facet_side // 2
    gain_wide = jnp.tile(beam[0].astype(jnp.float32), (1, taylor_count))
    weighted = (model.astype(jnp.float32) * gain_wide).astype(jnp.bfloat16)
    u_shift = uv_offsets[0, 0, 0]
    v_shift = uv_offsets[0, 0, 1]
    w_shift = w_planes[0, 0]
    ev_rows = []
    ev_cols = []
    for sub_index in range(sub_count):
        ev_real, ev_imag = axis_table(
            v_shift[sub_index] + cell_index, m_pixels, w_shift[sub_index], facet_side
        )
        ev_rows = ev_rows + [ev_real, ev_imag]
        ev_cols.append(jnp.concatenate([ev_real, ev_imag], axis=1))
    ev_stack = jnp.concatenate(ev_rows, axis=0)

    def eu_tables(row_count):
        l_pixels = jnp.arange(row_count, dtype=jnp.int32) - extent // 2
        tables = []
        for sub_index in range(sub_count):
            eu_real, eu_imag = axis_table(
                u_shift[sub_index] + cell_index, l_pixels, w_shift[sub_index], extent
            )
            tables.append(jnp.concatenate([eu_real, eu_imag], axis=0))
        return tables

    shard_rows = lax.all_gather(weighted, "vis", axis=0, tiled=True)
    row_count = shard_rows.shape[0]
    projected = lax.dot_general(
        shard_rows.reshape(row_count * taylor_count, facet_side),
        ev_stack,
        (((1,), (1,)), ((), ())),
        preferred_element_type=jnp.float32,
    ).astype(jnp.bfloat16)
    projected = projected.reshape(row_count, taylor_count, sub_count, 2 * S)
    tables = eu_tables(row_count)
    updated = []
    for fold_sub_index in range(sub_count):
        updated.append(
            jnp.dot(
                tables[fold_sub_index],
                projected[:, :, fold_sub_index, :].reshape(row_count, taylor_count * 2 * S),
                preferred_element_type=jnp.float32,
            )
        )
    grid_sums = tuple(updated)
    u_frac = vis_uv[0, 0, 0]
    v_frac = vis_uv[0, 0, 1]
    spectrum = spectral[0, 0]
    sub_ids = vis_subgrid[0, 0]
    powers = jnp.stack([spectrum**term_index for term_index in range(taylor_count)])
    live_mask = (jnp.arange(vis_count, dtype=jnp.int32) < counts[0, 0]).astype(jnp.float32)
    predicted = jnp.zeros((2, vis_count), jnp.float32)
    ku_all = []
    kv_all = []
    for sub_index in range(sub_count):
        product = grid_sums[sub_index].reshape(2, S, taylor_count, 2, S)
        model_grid = jnp.stack(
            [product[0, :, :, 0] - product[1, :, :, 1], product[0, :, :, 1] + product[1, :, :, 0]]
        ).astype(jnp.bfloat16)
        members = (sub_ids == sub_index).astype(jnp.float32)
        ku_table = kernel_table(u_frac, members, S)
        kv_table = kernel_table(v_frac, members, S)
        cell_wide = jnp.dot(
            model_grid.reshape(2 * S * taylor_count, S),
            kv_table,
            preferred_element_type=jnp.float32,
        ).reshape(2, S, taylor_count, vis_count)
        ku_wide = ku_table.astype(jnp.float32)[None, :, None, :] * powers[None, None, :, :]
        predicted = predicted + jnp.sum(cell_wide * ku_wide, axis=(1, 2))
        ku_all.append(ku_wide)
        kv_all.append(kv_table)
    residual = live_mask[None, :] * (vis_obs[0, 0] - predicted)
    sections = []
    for sub_index in range(sub_count):
        spread = (residual[:, None, None, :] * ku_all[sub_index]).astype(jnp.bfloat16)
        spread = spread.reshape(2 * S * taylor_count, vis_count)
        cell_sum = lax.dot_general(
            spread, kv_all[sub_index], (((1,), (1,)), ((), ())), preferred_element_type=jnp.float32
        ).astype(jnp.bfloat16)
        side_prod = jnp.dot(
            cell_sum, ev_cols[sub_index], preferred_element_type=jnp.float32
        ).reshape(2, S, taylor_count, 2, facet_side)
        back = jnp.stack(
            [
                side_prod[0, :, :, 0] + side_prod[1, :, :, 1],
                side_prod[1, :, :, 0] - side_prod[0, :, :, 1],
            ]
        ).astype(jnp.bfloat16)
        sections.append(back.reshape(2 * S, taylor_count * facet_side))
    section_stack = jnp.concatenate(sections, axis=0)
    tables = jnp.concatenate(eu_tables(extent), axis=0)
    image_sum = lax.psum(
        lax.dot_general(
            tables, section_stack, (((0,), (0,)), ((), ())), preferred_element_type=jnp.float32
        )
        * norm_scale,
        "vis",
    )
    owned = lax.dynamic_slice_in_dim(image_sum, lax.axis_index("vis") * rows_own, rows_own, 0)
    weighted_image = gain_wide * owned
    dirty = lax.psum(weighted_image, "freq")
    return (residual.reshape(1, 1, 2, vis_count), dirty)


def solution(mesh):
    in_specs = (
        P("vis", None),
        P("freq", "vis", None),
        P("freq", "vis", None, None),
        P("freq", "vis", None, None),
        P("freq", "vis", None),
        P("freq", "vis", None),
        P("freq", "vis"),
        P("freq", "vis", None, None),
        P("freq", "vis", None),
    )
    out_specs = (P("freq", "vis", None, None), P("vis", None))
    return jax.shard_map(shards, mesh=mesh, in_specs=in_specs, out_specs=out_specs, check_vma=False)
```

profile of v0, /device:TPU:1, one launch (start us, length us, event | category | flops | bytes accessed | tf_op | source)
XLA Modules:
  0.0 701.4 jit_solution(16787390874322196959)
XLA Ops:
  7.9 1.5 multiply_convert_fusion.12
  10.2 1.3 fusion.109
  12.1 1.5 fusion.108
  15.7 1.1 fusion.89
  16.9 1.4 fusion.78
  20.2 2.3 cosine_convert_fusion.1
  25.8 1.9 broadcast_multiply_fusion
  27.7 129.8 %all-gather.2.cloned.1.call-done = bf16[256,4096]{1,0:T(8,128)(2,1)} async-done(((bf16[8,4096]{1,0:T(8,128)(2,1)}), bf16[256,4096]{1,0:T(8,128)(2,1)}) %all-gather.2.cloned.1.call-update) | async-done | bytes 2097168 | tf_op jit(solution)/shard_map/all_gather | solution.py:68
  157.5 4.4 reshape.491
  161.9 2.3 convolution_convert_fusion
  164.3 1.5 fusion.106
  165.8 1.3 copy.59
  169.1 2.3 multiply_reduce_fusion.1
  173.1 2.0 multiply_convert_fusion.1
  175.1 3.0 copy.49
  178.1 2.6 convert_element_type.225
  180.7 3.5 fusion.4
  184.2 6.7 reshape.494
  190.8 8.7 %fusion.105 = (f32[1,64,4,1,1024]{4,3,2,1,0:T(1,128)S(1)}, f32[1,64,4,1,1024]{4,3,2,1,0:T(1,128)S(1)}, f32[1,64,4,1,1024]{4,3,2,1,0:T(1,128)S(1)}, f32[1,64,4,1,1024]{4,3,2,1,0:T(1,128)S(1)}) fusion(f32[2,64,4,2,1024]{4,3,2,1,0:T(2,128)} %reshape.494), kind=kLoop, calls=%fused_computation.191 | loop fusion | bytes 8388608 | tf_op jit(solution)/shard_map/slice | solution.py:127
  199.6 1.1 fusion.12
  200.7 1.1 fusion.11
  203.5 3.0 copy.43
  206.5 2.5 convert_element_type.221
  209.0 3.5 fusion.3
  212.5 6.7 reshape.493
  219.2 8.7 %fusion.104 = (f32[1,64,4,1,1024]{4,3,2,1,0:T(1,128)S(1)}, f32[1,64,4,1,1024]{4,3,2,1,0:T(1,128)S(1)}, f32[1,64,4,1,1024]{4,3,2,1,0:T(1,128)S(1)}, f32[1,64,4,1,1024]{4,3,2,1,0:T(1,128)S(1)}) fusion(f32[2,64,4,2,1024]{4,3,2,1,0:T(2,128)} %reshape.493), kind=kLoop, calls=%fused_computation.190 | loop fusion | bytes 8388608 | tf_op jit(solution)/shard_map/slice | solution.py:127
  227.9 1.1 fusion.10
  231.5 2.8 convolution_multiply_fusion
  234.4 310.4 %all-reduce.3.cloned.1.call-done = f32[256,4096]{1,0:T(8,128)} async-done(((f32[256,4096]{1,0:T(8,128)}), f32[256,4096]{1,0:T(8,128)}) %all-reduce.3.cloned.1.call-update) | async-done | bytes 4194320 | tf_op jit(solution)/shard_map/psum | solution.py:134
  544.7 1.6 dynamic-slice_multiply_fusion
  547.0 146.3 %all-reduce.5.cloned.1.call-done = f32[8,4096]{1,0:T(8,128)} async-done(((f32[8,4096]{1,0:T(8,128)}), f32[8,4096]{1,0:T(8,128)}) %all-reduce.5.cloned.1.call-update) | async-done | bytes 131088 | tf_op jit(solution)/shard_map/psum | solution.py:143
  693.3 1.6 copy.110
  (91 shorter events, 17.1 us)
Async XLA Ops:
  7.2 150.3 %all-gather.2.cloned.1.call-start = ((), (), s32[]{:S(2)}) async-start(), calls=%async_computation | async-start | bytes 2162688 | tf_op jit(solution)/shard_map/all_gather | solution.py:68
  9.5 535.3 %all-reduce.3.cloned.1.call-start = ((), (), s32[]{:S(2)}) async-start(), calls=%async_computation.1 | async-start | bytes 8388608 | tf_op jit(solution)/shard_map/psum | solution.py:134
  19.5 6.1 copy-start.6
  19.5 6.1 copy-start.8
  19.5 6.1 copy-start.10
  19.5 6.1 copy-start.12
  22.5 139.3 %copy-start.2 = (bf16[64,1024]{1,0:T(8,128)(2,1)}, bf16[64,1024]{1,0:T(8,128)(2,1)S(1)}, u32[]{:S(2)}) copy-start(bf16[64,1024]{1,0:T(8,128)(2,1)S(1)} %get-tuple-element.28) | copy-start | bytes 393220
  22.5 139.3 %copy-start.4 = (bf16[64,1024]{1,0:T(8,128)(2,1)}, bf16[64,1024]{1,0:T(8,128)(2,1)S(1)}, u32[]{:S(2)}) copy-start(bf16[64,1024]{1,0:T(8,128)(2,1)S(1)} %get-tuple-element.29) | copy-start | bytes 393220
  23.3 4.4 copy-start.19
  165.8 2.9 copy-start.14
  169.1 2.4 copy-start.20
  171.4 0.8 copy-start.15
  171.5 0.8 copy-start.21
  171.5 0.8 copy-start.23
  171.5 1.6 copy-start
  172.3 2.8 copy-start.17
  178.1 2.6 copy-start.3
  178.1 2.6 copy-start.5
  201.9 1.6 copy-start.1
  230.2 1.2 copy-start.7
  230.2 1.2 copy-start.9
  230.2 1.2 copy-start.11
  230.3 1.2 copy-start.13
  234.3 312.0 %copy-start.16 = (f32[2,2048]{1,0:T(2,128)S(1)}, f32[2,2048]{1,0:T(2,128)}, u32[]{:S(2)}) copy-start(f32[2,2048]{1,0:T(2,128)} %copy-done.15) | copy-start | bytes 49156
  234.3 312.1 %copy-start.18 = (f32[2,2048]{1,0:T(2,128)S(1)}, f32[2,2048]{1,0:T(2,128)}, u32[]{:S(2)}) copy-start(f32[2,2048]{1,0:T(2,128)} %copy-done.17) | copy-start | bytes 49156
  234.3 312.1 %copy-start.22 = (f32[2048]{0:T(1024)S(1)}, f32[2048]{0:T(1024)}, u32[]{:S(2)}) copy-start(f32[2048]{0:T(1024)} %fusion.75) | copy-start | bytes 24580
  234.3 312.1 %copy-start.24 = (f32[1,1,2,2048]{3,2,1,0:T(2,128)S(1)}, f32[1,1,2,2048]{3,2,1,0:T(2,128)}, u32[]{:S(2)}) copy-start(f32[1,1,2,2048]{3,2,1,0:T(2,128)} %param.11) | copy-start | bytes 49156
  234.3 459.0 %all-reduce.5.cloned.1.call-start = ((), (), s32[]{:S(2)}) async-start(), calls=%async_computation.2 | async-start | bytes 262144 | tf_op jit(solution)/shard_map/psum | solution.py:143
Sparse Core Ops, SparseCore 0:
  11.1 146.3 all-gather.1
  234.4 310.2 all-reduce.2
  548.2 145.0 all-reduce.4
where the time goes:
time: 703 us; the launch traced here: 701 us
  waiting for transfers between devices  587 us (83%)
  local copies, waits for them, and re-layouts  58.4 us (8%)
  other arithmetic  24.9 us (4%)
  matrix products  16.4 us (2%)
  between operations  15 us (2%)
    psum x1, waiting for transfers between devices, shards(): lax.psum(lax.dot_general(tables, section_stack, (((0,), (0,)), ((), ())),...  310 us
    psum x1, waiting for transfers between devices, shards(): dirty = lax.psum(weighted_image, 'freq')  146 us
    all_gather x1, waiting for transfers between devices, shards(): shard_rows = lax.all_gather(weighted, 'vis', axis=0, tiled=True)  130 us
    slice x2, local copies, waits for them, and re-layouts, shards(): side_prod[0, :, :, 0] + side_prod[1, :, :, 1]  17.4 us
  transfers between devices with their start and end apart: 3, of which 3 were waited for; matrix products, arithmetic and copies ran while one was open for 3% of the time, Pallas kernels for 0%

commit v1 on v0

v1 whole, which is shorter than its diff:
```python
import functools
import math

import jax
import jax.numpy as jnp
import numpy as np
from jax import lax
from jax.experimental import pallas as pl
from jax.experimental.pallas import tpu as pltpu
from jax.sharding import PartitionSpec as P

S = 64
KERNEL_WIDTH = 0.5
MESH = pl.DeviceIdType.MESH


def greet(axis, n, me):
    barrier = pltpu.get_barrier_semaphore()

    def one(d, carry):
        pl.semaphore_signal(
            barrier, inc=1, device_id={axis: lax.rem(me + d, n)}, device_id_type=MESH
        )
        return carry

    lax.fori_loop(1, n, one, 0)
    pl.semaphore_wait(barrier, n - 1)


def exchange_kernel(axis, n, spread, in_ref, out_ref, send_sem, recv_sem, own_sem):
    me = lax.axis_index(axis)

    def copy(d):
        to = lax.rem(me + d, n)
        return pltpu.make_async_remote_copy(
            src_ref=in_ref.at[to] if spread else in_ref,
            dst_ref=out_ref.at[me],
            send_sem=send_sem.at[d],
            recv_sem=recv_sem.at[d],
            device_id={axis: to},
            device_id_type=MESH,
        )

    greet(axis, n, me)

    def begin(d, carry):
        copy(d).start()
        return carry

    lax.fori_loop(1, n, begin, 0)
    own = pltpu.make_async_copy(in_ref.at[me] if spread else in_ref, out_ref.at[me], own_sem)
    own.start()
    own.wait()

    def end(d, carry):
        frm = lax.rem(me - d + n, n)
        got = pltpu.make_async_remote_copy(
            src_ref=in_ref.at[frm] if spread else in_ref,
            dst_ref=out_ref.at[frm],
            send_sem=send_sem.at[d],
            recv_sem=recv_sem.at[d],
            device_id={axis: frm},
            device_id_type=MESH,
        )
        got.wait_recv()
        copy(d).wait_send()
        return carry

    lax.fori_loop(1, n, end, 0)


def exchange(array, axis, spread, collective_id):
    n = lax.axis_size(axis)
    block = array.shape[1:] if spread else array.shape
    return pl.pallas_call(
        functools.partial(exchange_kernel, axis, n, spread),
        out_shape=jax.ShapeDtypeStruct((n,) + block, array.dtype),
        in_specs=[pl.BlockSpec(memory_space=pltpu.VMEM)],
        out_specs=pl.BlockSpec(memory_space=pltpu.VMEM),
        scratch_shapes=[
            pltpu.SemaphoreType.DMA((n,)),
            pltpu.SemaphoreType.DMA((n,)),
            pltpu.SemaphoreType.DMA,
        ],
        compiler_params=pltpu.CompilerParams(
            collective_id=collective_id, has_side_effects=True
        ),
    )(array)


def freq_sum_kernel(n, in_ref, out_ref, parts, total, send_sem, recv_sem, send2, recv2, own_sem):
    me = lax.axis_index("freq")
    greet("freq", n, me)

    def first(d, to):
        return pltpu.make_async_remote_copy(
            src_ref=in_ref.at[to],
            dst_ref=parts.at[d],
            send_sem=send_sem.at[d],
            recv_sem=recv_sem.at[d],
            device_id={"freq": to},
            device_id_type=MESH,
        )

    def second(d, to, slot):
        return pltpu.make_async_remote_copy(
            src_ref=total,
            dst_ref=out_ref.at[slot],
            send_sem=send2.at[d],
            recv_sem=recv2.at[d],
            device_id={"freq": to},
            device_id_type=MESH,
        )

    def begin(d, carry):
        first(d, lax.rem(me + d, n)).start()
        return carry

    lax.fori_loop(1, n, begin, 0)
    total[...] = in_ref[me]

    def take(d, carry):
        first(d, lax.rem(me - d + n, n)).wait_recv()
        total[...] += parts[d]
        return carry

    lax.fori_loop(1, n, take, 0)

    def tell(d, carry):
        second(d, lax.rem(me + d, n), me).start()
        return carry

    lax.fori_loop(1, n, tell, 0)
    own = pltpu.make_async_copy(total, out_ref.at[me], own_sem)
    own.start()
    own.wait()

    def end(d, carry):
        frm = lax.rem(me - d + n, n)
        second(d, frm, frm).wait_recv()
        second(d, lax.rem(me + d, n), me).wait_send()
        first(d, lax.rem(me + d, n)).wait_send()
        return carry

    lax.fori_loop(1, n, end, 0)


def freq_sum(array, collective_id):
    n = array.shape[0]
    block = array.shape[1:]
    dma = pltpu.SemaphoreType.DMA
    return pl.pallas_call(
        functools.partial(freq_sum_kernel, n),
        out_shape=jax.ShapeDtypeStruct(array.shape, array.dtype),
        in_specs=[pl.BlockSpec(memory_space=pltpu.VMEM)],
        out_specs=pl.BlockSpec(memory_space=pltpu.VMEM),
        scratch_shapes=[
            pltpu.VMEM((n,) + block, array.dtype),
            pltpu.VMEM(block, array.dtype),
            dma((n,)),
            dma((n,)),
            dma((n,)),
            dma((n,)),
            dma,
        ],
        compiler_params=pltpu.CompilerParams(
            collective_id=collective_id, has_side_effects=True
        ),
    )(array)


def unit(turns):
    phases = -2.0 * math.pi * turns
    return jnp.cos(phases), jnp.sin(phases)


def dft_tables(pixels):
    cells = np.arange(S) - S // 2
    places = np.arange(pixels) - pixels // 2
    angle = -2.0 * np.pi * np.mod(cells[:, None] * places[None, :], pixels) / pixels
    return np.cos(angle).astype(np.float32), np.sin(angle).astype(np.float32)


def ramp(shift, w_plane, pixels):
    places = jnp.arange(pixels, dtype=jnp.int32) - pixels // 2
    linear = jnp.mod(shift[..., None] * places, pixels).astype(jnp.float32) / pixels
    wrap = 2 * pixels * pixels
    quadratic = jnp.mod(w_plane[..., None] * places * places, wrap).astype(jnp.float32) / wrap
    return linear + quadratic


def kernel_table(position):
    cell_pos = jnp.arange(S, dtype=jnp.float32)
    offset_cells = position[None, :] - cell_pos[:, None]
    values = jnp.exp(offset_cells * offset_cells * (-0.5 / (KERNEL_WIDTH * KERNEL_WIDTH)))
    return values.astype(jnp.bfloat16)


def shards(model, beam, vis_obs, vis_uv, spectral, vis_subgrid, counts, uv_offsets, w_planes):
    rows_own = model.shape[0]
    fs = beam.shape[-1]
    tay = model.shape[1] // fs
    blocks = lax.axis_size("vis")
    groups = lax.axis_size("freq")
    extent = rows_own * blocks
    ns = w_planes.shape[-1]
    nv = vis_obs.shape[-1]
    norm_scale = 1.0 / (S * math.sqrt(groups * blocks * ns))
    rt = tay * rows_own
    bf = jnp.bfloat16
    f32 = jnp.float32

    gain = beam[0].astype(f32)
    model_t = model.reshape(rows_own, tay, fs).transpose(1, 0, 2).astype(f32)
    weighted = (model_t * gain[None]).astype(bf).reshape(rt, fs).astype(f32)

    tile = jnp.concatenate([uv_offsets[0, 0, 1], w_planes[0, 0]]).astype(f32)
    tile = jnp.broadcast_to(jnp.pad(tile, (0, 8 - 2 * ns))[:, None], (8, 128))
    tiles = exchange(tile, "vis", False, 0)
    facts = tiles[:, : 2 * ns, 0].astype(jnp.int32)
    turns = ramp(facts[:, :ns], facts[:, ns:], fs)
    r_re, r_im = unit(turns)

    t_re, t_im = dft_tables(fs)
    t_fwd = np.concatenate(
        [np.concatenate([t_re.T, t_im.T], 1), np.concatenate([-t_im.T, t_re.T], 1)], 0
    )
    t_fwd = jnp.asarray(t_fwd, bf)
    x = jnp.concatenate(
        [weighted * r_re[:, :, None, :], weighted * r_im[:, :, None, :]], axis=-1
    ).astype(bf)
    proj = jnp.dot(x.reshape(blocks * ns * rt, 2 * fs), t_fwd, preferred_element_type=f32)
    proj = proj.reshape(blocks, ns, rt, 2, S).transpose(0, 2, 3, 1, 4)
    proj = proj.reshape(blocks, rt, 2 * ns * S).astype(bf)
    got = exchange(proj, "vis", True, 1)

    l_pix = jnp.arange(extent, dtype=jnp.int32) - extent // 2
    cells = jnp.arange(S, dtype=jnp.int32) - S // 2
    eu = []
    for s in range(ns):
        lin = jnp.mod((uv_offsets[0, 0, 0, s] + cells)[:, None] * l_pix[None, :], extent)
        wrap = 2 * extent * extent
        quad = jnp.mod(w_planes[0, 0, s] * l_pix * l_pix, wrap)
        eu += unit(lin.astype(f32) / extent + (quad.astype(f32) / wrap)[None, :])
    eu = jnp.concatenate(eu, axis=0).astype(bf)

    width = 2 * ns * S
    got = got.reshape(blocks, tay, rows_own, width).transpose(1, 0, 2, 3).reshape(tay, extent, width)
    prod = jnp.einsum("ar,trn->tan", eu, got, preferred_element_type=f32)
    prod = prod.reshape(tay, ns, 2, S, 2, ns, S)
    grid_re = jnp.stack(
        [prod[:, s, 0, :, 0, s] - prod[:, s, 1, :, 1, s] for s in range(ns)], axis=2
    )
    grid_im = jnp.stack(
        [prod[:, s, 0, :, 1, s] + prod[:, s, 1, :, 0, s] for s in range(ns)], axis=2
    )
    grid = jnp.stack([grid_re, grid_im]).astype(bf).reshape(2 * tay * S, ns * S)

    ku = kernel_table(vis_uv[0, 0, 0]).astype(f32)
    kv = kernel_table(vis_uv[0, 0, 1])
    sub = vis_subgrid[0, 0]
    kv = jnp.concatenate([jnp.where(sub[None, :] == s, kv, 0) for s in range(ns)], axis=0).astype(bf)
    spectrum = spectral[0, 0]
    powers = jnp.stack([spectrum**t for t in range(tay)])
    cell = jnp.dot(grid, kv, preferred_element_type=f32).reshape(2, tay, S, nv)
    predicted = jnp.sum(jnp.sum(cell * ku[None, None], axis=2) * powers[None], axis=1)
    live = (jnp.arange(nv, dtype=jnp.int32) < counts[0, 0]).astype(f32)
    residual = live[None] * (vis_obs[0, 0] - predicted)
    spread = ((residual[:, None] * powers[None])[:, :, None] * ku[None, None]).astype(bf)
    rg = lax.dot_general(
        spread.reshape(2 * tay * S, nv), kv, (((1,), (1,)), ((), ())), preferred_element_type=f32
    ).astype(bf)
    rg = rg.reshape(2, tay, S, ns, S)
    zero = jnp.zeros((tay, S, S), bf)
    rows = []
    for s in range(ns):
        re, im = rg[0, :, :, s], rg[1, :, :, s]
        pad = lambda v: [v if k == s else zero for k in range(ns)]
        rows.append(jnp.concatenate(pad(re) + pad(im), axis=-1))
        rows.append(jnp.concatenate(pad(im) + pad(-re), axis=-1))
    rhs = jnp.concatenate(rows, axis=1)
    h = jnp.einsum("ar,tan->trn", eu, rhs, preferred_element_type=f32).astype(bf)
    h = h.reshape(tay, blocks, rows_own, width).transpose(1, 0, 2, 3).reshape(blocks, rt, width)
    back = exchange(h, "vis", True, 2)

    t_bwd = np.zeros((2, ns, S, ns, 2, fs), np.float32)
    for s in range(ns):
        t_bwd[0, s, :, s, 0] = t_re
        t_bwd[1, s, :, s, 0] = t_im
        t_bwd[0, s, :, s, 1] = -t_im
        t_bwd[1, s, :, s, 1] = t_re
    t_bwd = jnp.asarray(t_bwd.reshape(width, ns * 2 * fs), bf)
    z = jnp.dot(back.reshape(blocks * rt, width), t_bwd, preferred_element_type=f32)
    z = z.reshape(blocks, rt, ns, 2, fs)
    term = jnp.sum(
        z[:, :, :, 0] * r_re[:, None] + z[:, :, :, 1] * r_im[:, None], axis=(0, 2)
    )
    image = term.reshape(tay, rows_own, fs) * (gain * norm_scale)[None]
    image = image.transpose(1, 0, 2).reshape(rows_own, groups, tay * fs // groups)
    dirty = freq_sum(image.transpose(1, 0, 2), 3)
    dirty = dirty.transpose(1, 0, 2).reshape(rows_own, tay * fs)
    return (residual.reshape(1, 1, 2, nv), dirty)


def solution(mesh):
    in_specs = (
        P("vis", None),
        P("freq", "vis", None),
        P("freq", "vis", None, None),
        P("freq", "vis", None, None),
        P("freq", "vis", None),
        P("freq", "vis", None),
        P("freq", "vis"),
        P("freq", "vis", None, None),
        P("freq", "vis", None),
    )
    out_specs = (P("freq", "vis", None, None), P("vis", None))
    return jax.shard_map(shards, mesh=mesh, in_specs=in_specs, out_specs=out_specs, check_vma=False)
```

time: 703 us -> 166 us (0.24)
  waiting for transfers between devices: 587 us -> 0 us
  Pallas kernels: 0 us -> 113 us
  local copies, waits for them, and re-layouts: 58.4 us -> 17.8 us
  between operations: 15 us -> 1.93 us
  matrix products: 16.4 us -> 9.21 us
    psum x2 -> x0, waiting for transfers between devices: 457 us -> none  [the longest x1 310 us: shards(): lax.psum(lax.dot_general(tables, section_stack, (((0,), (0,)), ((), ())),...]
    all_gather x1 -> x0, waiting for transfers between devices: 130 us -> none  [shards(): shard_rows = lax.all_gather(weighted, 'vis', axis=0, tiled=True)]
    pallas_call x0 -> x4, Pallas kernels: none -> 113 us  [the longest x3 94.3 us: exchange(): pl.pallas_call(functools.partial(exchange_kernel, axis, n, spread), out_s...]
    slice x6 -> x8, local copies, waits for them, and re-layouts: 22.6 us -> 5.85 us  [the longest x1 1.77 us: shards(): prod[:, s, 1, :, 1, s]]
    reshape x4 -> x3, local copies, waits for them, and re-layouts: 17.8 us -> 2.24 us  [the longest x1 1.24 us: shards(): prod = prod.reshape(tay, ns, 2, S, 2, ns, S)]
    convert_element_type x4 -> x3, local copies, waits for them, and re-layouts: 11.1 us -> 2.65 us  [the longest x2 2.55 us: shards(): proj = proj.reshape(blocks, rt, 2 * ns * S).astype(bf)]
    dot_general x8 -> x6, matrix products: 16.4 us -> 9.21 us  [the longest x1 3.46 us: shards(): jnp.dot(back.reshape(blocks * rt, width), t_bwd, preferred_element_type=f32)]
  transfers between devices with their start and end apart: 3 -> 0, of which waited for: 3 -> 0; matrix products, arithmetic and copies ran while one was open for 3% -> 0% of each run, Pallas kernels for 0% -> 0%
where the time goes in v1:
time: 166 us; the launch traced here: 163 us
  Pallas kernels  113 us (68%)
  other arithmetic  22 us (13%)
  local copies, waits for them, and re-layouts  17.8 us (11%)
  matrix products  9.21 us (6%)
  between operations  1.93 us (1%)
    pallas_call x3, Pallas kernels, exchange(): pl.pallas_call(functools.partial(exchange_kernel, axis, n, spread), out_s...  94.3 us
    pallas_call x1, Pallas kernels, freq_sum(): pl.pallas_call(functools.partial(freq_sum_kernel, n), out_shape=jax.Shape...  18.3 us
    unnamed x47, local copies, waits for them, and re-layouts  5.2 us
    cos x1, other arithmetic, unit(): return (jnp.cos(phases), jnp.sin(phases))  5.01 us
    another operation x2, other arithmetic  3.61 us
    dot_general x1, matrix products, shards(): jnp.dot(back.reshape(blocks * rt, width), t_bwd, preferred_element_type=f32)  3.46 us

profile of v1, /device:TPU:1, one launch (start us, length us, event | category | flops | bytes accessed | tf_op | source)
XLA Modules:
  0.0 163.5 jit_solution(15940342846073008689)
XLA Ops:
  0.6 0.8 fusion.96
  1.4 0.9 fusion.53
  2.3 0.8 compare_reduce_fusion.1
  3.1 1.0 fusion.45
  4.1 1.3 fusion.99
  5.4 1.3 fusion.80
  6.7 1.3 fusion.98
  8.0 1.3 fusion.85
  10.7 0.7 add_convert_fusion.2
  12.1 25.5 %shard_map.122 = f32[32,8,128]{2,1,0:T(8,128)} custom-call(f32[8,128]{1,0:T(8,128)} %broadcast_in_dim.18.in_ref), custom_call_target="tpu_custom_call" | custom-call | tf_op jit(solution)/shard_map/pallas_call | solution.py:75
  37.6 0.9 slice_convert_fusion
  38.8 5.0 %fusion.60 = (f32[32,2,1024]{2,1,0:T(2,128)S(1)}, f32[32,2,1024]{2,1,0:T(2,128)S(1)}) fusion(s32[32,2]{1,0:T(8,128)S(1)} %copy.56, s32[1024]{0:T(1024)S(1)} %iota_add_fusion, s32[32,2]{1,0:T(8,128)S(1)} %copy.55), kind=kLoop, calls=%fused_computation.91 | loop fusion | flops 2031616 | bytes 528896 | tf_op jit(solution)/shard_map/cos | solution.py:174
  43.9 0.7 convert_bitcast_fusion.1
  44.6 0.9 convert_bitcast_fusion
  45.5 3.0 %multiply_convert_fusion.1 = (bf16[32,2,32,1024]{3,2,1,0:T(8,128)(2,1)S(1)}, bf16[32,2,32,1024]{3,2,1,0:T(8,128)(2,1)S(1)}) fusion(f32[32,2,1024]{2,1,0:T(2,128)S(1)} %get-tuple-element.22, f32[32,1024]{1,0:T(8,128)S(1)} %convert_bitcast_fusion, f32[32,2,1024]{2,1,0:T(2,128)S(1)} %get-tuple-element.23), kind=kLoop, calls=%fused_computation.8 | loop fusion | flops 8388608 | bytes 9043968 | tf_op jit(solution)/shard_map/convert.19
  48.5 2.4 %fusion.6 = bf16[32,32,2,2,64]{4,1,2,3,0:T(8,128)(2,1)S(1)} fusion(bf16[2,64,2048,1,1]{2,1,0,4,3:T(8,128)(2,1)S(1)} %copy-done.17, bf16[32,2,32,1024]{3,2,1,0:T(8,128)(2,1)S(1)} %get-tuple-element.21, bf16[32,2,32,1024]{3,2,1,0:T(8,128)(2,1)S(1)} %get-tuple-element.20), kind=kOutput, calls=%fused_computation.13 | convolution fusion | flops 1090781184 | bytes 9437184 | tf_op jit(solution)/shard_map/dot_general | solution.py:232
  50.9 1.1 copy.57
  52.0 1.5 convert_element_type.166.in_ref
  53.4 37.7 %shard_map.123 = bf16[32,32,256]{2,1,0:T(8,128)(2,1)} custom-call(bf16[32,32,256]{2,1,0:T(8,128)(2,1)} %convert_element_type.166.in_ref), custom_call_target="tpu_custom_call" | custom-call | tf_op jit(solution)/shard_map/pallas_call | solution.py:75
  91.1 1.4 convolution_bitcast_fusion
  92.5 1.2 reshape.378
  93.8 1.8 %fusion.94 = (f32[4,1,1,64,1,1,64]{3,2,1,6,5,4,0:T(1,128)S(1)}, f32[4,1,1,64,1,1,64]{3,2,1,6,5,4,0:T(1,128)}, f32[4,1,1,64,1,1,64]{3,2,1,6,5,4,0:T(1,128)S(1)}, ...) fusion(f32[4,2,2,64,2,2,64]{3,2,1,6,5,4,0:T(2,128)S(1)} %reshap, ...), kind=kLoop, calls=%fused_computation.169 | loop fusion | bytes 1048576 | tf_op jit(solution)/shard_map/slice | solution.py:252
  95.6 1.1 copy.90
  96.6 1.0 copy.91
  97.7 1.0 copy.88
  102.5 0.7 convolution_convert_fusion.1
  104.6 0.9 copy.108
  105.4 31.1 %shard_map.124 = bf16[32,32,256]{2,1,0:T(8,128)(2,1)} custom-call(bf16[32,32,256]{2,1,0:T(8,128)(2,1)} %bitcast.137), custom_call_target="tpu_custom_call" | custom-call | tf_op jit(solution)/shard_map/pallas_call | solution.py:75
  136.6 3.5 %fusion.39 = f32[32,32,2,2,1024]{4,1,3,2,0:T(8,128)S(1)} fusion(bf16[2,2,1024,256,1]{3,2,1,0,4:T(8,128)(2,1)S(1)} %copy-done.3, bf16[32,32,256]{2,1,0:T(8,128)(2,1)} %shard_map.124), kind=kOutput, calls=%fused_computation.54 | convolution fusion | flops 2147483648 | bytes 19398656 | tf_op jit(solution)/shard_map/dot_general | solution.py:293
  140.1 2.9 %fusion.2 = f32[32,1024]{1,0:T(8,128)S(1)} fusion(f32[32,32,2,2,1024]{4,1,3,2,0:T(8,128)S(1)} %fusion.39, f32[32,2,1024]{2,1,0:T(2,128)S(1)} %copy-done.1, f32[32,2,1024]{2,1,0:T(2,128)S(1)} %get-tuple-element.22), kind=kLoop, calls=%fused_computation.3 | loop fusion | flops 8355840 | bytes 17432576 | tf_op jit(solution)/shard_map/reduce_sum | solution.py:295
  143.7 18.3 %shard_map.125 = f32[16,8,256]{2,1,0:T(8,128)} custom-call(f32[16,8,256]{2,1,0:T(8,128)} %bitcast.138), custom_call_target="tpu_custom_call" | custom-call | tf_op jit(solution)/shard_map/pallas_call | solution.py:152
  161.9 1.6 copy.113
  (81 shorter events, 7.2 us)
Async XLA Ops:
  10.0 81.1 %copy-start.6 = (bf16[64,256]{1,0:T(8,128)(2,1)}, bf16[64,256]{1,0:T(8,128)(2,1)S(1)}, u32[]{:S(2)}) copy-start(bf16[64,256]{1,0:T(8,128)(2,1)S(1)} %get-tuple-element.30) | copy-start | bytes 98308
  10.0 81.1 %copy-start.8 = (bf16[64,256]{1,0:T(8,128)(2,1)}, bf16[64,256]{1,0:T(8,128)(2,1)S(1)}, u32[]{:S(2)}) copy-start(bf16[64,256]{1,0:T(8,128)(2,1)S(1)} %get-tuple-element.31) | copy-start | bytes 98308
  10.0 81.1 %copy-start.10 = (bf16[64,256]{1,0:T(8,128)(2,1)}, bf16[64,256]{1,0:T(8,128)(2,1)S(1)}, u32[]{:S(2)}) copy-start(bf16[64,256]{1,0:T(8,128)(2,1)S(1)} %get-tuple-element.36) | copy-start | bytes 98308
  10.0 81.1 %copy-start.12 = (bf16[64,256]{1,0:T(8,128)(2,1)}, bf16[64,256]{1,0:T(8,128)(2,1)S(1)}, u32[]{:S(2)}) copy-start(bf16[64,256]{1,0:T(8,128)(2,1)S(1)} %get-tuple-element.37) | copy-start | bytes 98308
  43.9 4.6 %copy-start = (f32[32,2,1024]{2,1,0:T(2,128)}, f32[32,2,1024]{2,1,0:T(2,128)S(1)}, u32[]{:S(2)}) copy-start(f32[32,2,1024]{2,1,0:T(2,128)S(1)} %get-tuple-element.23) | copy-start | bytes 786436
  45.5 3.0 %copy-start.17 = (bf16[2,64,2048,1,1]{2,1,0,4,3:T(8,128)(2,1)S(1)}, bf16[2,64,2048,1,1]{2,1,0,4,3:T(8,128)(2,1)}, u32[]{:S(2)}) copy-start(bf16[2,64,2048,1,1]{2,1,0,4,3:T(8,128)(2,1)} %constant.131) | copy-start | bytes 1572868
  93.8 6.1 %copy-start.2 = (f32[64,2048]{1,0:T(8,128)S(1)}, f32[64,2048]{1,0:T(8,128)}, u32[]{:S(2)}) copy-start(f32[64,2048]{1,0:T(8,128)} %fusion.53) | copy-start | bytes 1572868
  95.6 4.3 %copy-start.4 = (bf16[64,2048]{1,0:T(8,128)(2,1)S(1)}, bf16[64,2048]{1,0:T(8,128)(2,1)}, u32[]{:S(2)}) copy-start(bf16[64,2048]{1,0:T(8,128)(2,1)} %get-tuple-element.28) | copy-start | bytes 786436
  95.6 4.3 %copy-start.5 = (bf16[64,2048]{1,0:T(8,128)(2,1)S(1)}, bf16[64,2048]{1,0:T(8,128)(2,1)}, u32[]{:S(2)}) copy-start(bf16[64,2048]{1,0:T(8,128)(2,1)} %get-tuple-element.29) | copy-start | bytes 786436
  95.6 5.0 %copy-start.16 = (f32[1,1,2048]{2,1,0:T(1,128)S(1)}, f32[1,1,2048]{2,1,0:T(1,128)}, u32[]{:S(2)}) copy-start(f32[1,1,2048]{2,1,0:T(1,128)} %param.15) | copy-start | bytes 24580
  95.6 5.9 %copy-start.14 = (f32[1,1,2,2048]{3,2,1,0:T(2,128)S(1)}, f32[1,1,2,2048]{3,2,1,0:T(2,128)}, u32[]{:S(2)}) copy-start(f32[1,1,2,2048]{3,2,1,0:T(2,128)} %param.13) | copy-start | bytes 49156
  102.1 1.9 %copy-start.7 = (bf16[64,256]{1,0:T(8,128)(2,1)S(1)}, bf16[64,256]{1,0:T(8,128)(2,1)}, u32[]{:S(2)}) copy-start(bf16[64,256]{1,0:T(8,128)(2,1)} %copy-done.6) | copy-start | bytes 98308
  102.1 1.9 %copy-start.9 = (bf16[64,256]{1,0:T(8,128)(2,1)S(1)}, bf16[64,256]{1,0:T(8,128)(2,1)}, u32[]{:S(2)}) copy-start(bf16[64,256]{1,0:T(8,128)(2,1)} %copy-done.8) | copy-start | bytes 98308
  102.1 1.9 %copy-start.11 = (bf16[64,256]{1,0:T(8,128)(2,1)S(1)}, bf16[64,256]{1,0:T(8,128)(2,1)}, u32[]{:S(2)}) copy-start(bf16[64,256]{1,0:T(8,128)(2,1)} %copy-done.10) | copy-start | bytes 98308
  102.1 1.9 %copy-start.13 = (bf16[64,256]{1,0:T(8,128)(2,1)S(1)}, bf16[64,256]{1,0:T(8,128)(2,1)}, u32[]{:S(2)}) copy-start(bf16[64,256]{1,0:T(8,128)(2,1)} %copy-done.12) | copy-start | bytes 98308
  104.0 32.5 %copy-start.3 = (bf16[2,2,1024,256,1]{3,2,1,0,4:T(8,128)(2,1)S(1)}, bf16[2,2,1024,256,1]{3,2,1,0,4:T(8,128)(2,1)}, u32[]{:S(2)}) copy-start(bf16[2,2,1024,256,1]{3,2,1,0,4:T(8,128)(2,1)} %constant.132) | copy-start | bytes 6291460
  136.6 3.5 %copy-start.1 = (f32[32,2,1024]{2,1,0:T(2,128)S(1)}, f32[32,2,1024]{2,1,0:T(2,128)}, u32[]{:S(2)}) copy-start(f32[32,2,1024]{2,1,0:T(2,128)} %copy-done) | copy-start | bytes 786436
  140.0 2.9 %copy-start.15 = (bf16[1,8,1024]{2,1,0:T(8,128)(2,1)S(1)}, bf16[1,8,1024]{2,1,0:T(8,128)(2,1)}, u32[]{:S(2)}) copy-start(bf16[1,8,1024]{2,1,0:T(8,128)(2,1)} %param.12) | copy-start | bytes 49156

commit v2 on v0

v2 whole, which is shorter than its diff:
```python
import functools
import math

import jax
import jax.numpy as jnp
import numpy as np
from jax import lax
from jax.experimental import pallas as pl
from jax.experimental.pallas import tpu as pltpu
from jax.sharding import PartitionSpec as P

S = 64
KERNEL_WIDTH = 0.5
MESH = pl.DeviceIdType.MESH
BF = jnp.bfloat16
F32 = jnp.float32
I32 = jnp.int32


def dft_tables(pixels):
    cells = np.arange(S) - S // 2
    places = np.arange(pixels) - pixels // 2
    angle = -2.0 * np.pi * np.mod(cells[:, None] * places[None, :], pixels) / pixels
    return np.cos(angle).astype(np.float32), np.sin(angle).astype(np.float32)


def cos_of(phase, bits):
    full = 1 << bits
    phase = phase & (full - 1)
    phase = jnp.where(phase >= full // 2, full - phase, phase)
    x = (0.25 - phase.astype(F32) * (1.0 / full)) * (2.0 * math.pi)
    y = x * x
    total = jnp.full_like(x, -1.0 / math.factorial(11))
    for power in (9, 7, 5, 3, 1):
        sign = 1.0 if power % 4 == 1 else -1.0
        total = total * y + sign / math.factorial(power)
    return total * x


def phase_of(cell, place, w_plane, log2):
    pixels = 1 << log2
    linear = (cell * place) & (pixels - 1)
    quadratic = (w_plane * place * place) & (2 * pixels * pixels - 1)
    return (linear << (log2 + 1)) + quadratic


def offset(k):
    return ((k + 1) // 2) * (1 - 2 * ((k + 1) % 2))


def whole_kernel(
    dims,
    model_ref, beam_ref, obs_ref, uv_ref, spec_ref, sub_ref, counts_ref, off_ref, w_ref,
    fwd_hbm, bwd_hbm,
    res_ref, dirty_ref,
    t_fwd, t_bwd, mine, facts, ramps, weighted, xbuf, sends, got, stage, eu, eu_t, ku, kv,
    grid, gridded, h, back, image, parts, total,
    tab_sem, fact_s, fact_r, msg_s, msg_r, back_s, back_r, sum_s, sum_r, out_s, out_r,
):
    n, groups, tay, rows, fs, ns, nv = dims
    rt = tay * rows
    extent = n * rows
    log_fs = fs.bit_length() - 1
    log_ext = extent.bit_length() - 1
    lanes = 128
    qs = fs // lanes
    batch = 8
    me = lax.axis_index("vis")
    group = lax.axis_index("freq")
    half = ns * S

    def other(k):
        return lax.rem(me + offset(k) + n, n)

    def remote(src, dst, send, recv, axis, to):
        return pltpu.make_async_remote_copy(
            src_ref=src, dst_ref=dst, send_sem=send, recv_sem=recv,
            device_id={axis: to}, device_id_type=MESH,
        )

    def fact_copy(to, slot):
        return remote(mine, facts.at[slot], fact_s.at[to], fact_r.at[slot], "vis", to)

    def msg_copy(to, slot):
        return remote(sends.at[to], got.at[slot], msg_s.at[to], msg_r.at[slot], "vis", to)

    def back_copy(to, slot):
        return remote(sends.at[to], back.at[slot], back_s.at[to], back_r.at[slot], "vis", to)

    def sum_copy(to, slot):
        return remote(image.at[to], parts.at[slot], sum_s.at[to], sum_r.at[slot], "freq", to)

    width = tay * fs // groups

    def out_copy(to, slot):
        place = dirty_ref.at[:, pl.ds(pl.multiple_of(slot * width, lanes), width)]
        return remote(total, place, out_s.at[to], out_r.at[slot], "freq", to)

    fwd_copy = pltpu.make_async_copy(fwd_hbm, t_fwd, tab_sem.at[0])
    bwd_copy = pltpu.make_async_copy(bwd_hbm, t_bwd, tab_sem.at[1])
    fwd_copy.start()
    bwd_copy.start()
    barrier = pltpu.get_barrier_semaphore()

    def greet(axis, count, index):
        def one(d, carry):
            pl.semaphore_signal(
                barrier, inc=1, device_id={axis: lax.rem(index + d, count)}, device_id_type=MESH
            )
            return carry

        lax.fori_loop(1, count, one, 0)

    greet("vis", n, me)
    greet("freq", groups, group)

    lane = lax.broadcasted_iota(I32, (1, lanes), 1)
    fact = jnp.zeros((1, lanes), F32)
    for s in range(ns):
        fact = jnp.where(lane == s, off_ref[0, 0, 1, s].astype(F32), fact)
        fact = jnp.where(lane == ns + s, w_ref[0, 0, s].astype(F32), fact)
    mine[...] = fact
    gain = beam_ref[0].astype(F32)
    for t in range(tay):
        piece = (model_ref[:, t * fs : (t + 1) * fs].astype(F32) * gain).astype(BF)
        weighted[t * rows : (t + 1) * rows, :] = piece.astype(F32)

    pl.semaphore_wait(barrier, n - 1 + groups - 1)

    def tell(k, carry):
        fact_copy(other(k), me).start()
        return carry

    lax.fori_loop(1, n, tell, 0)
    facts[me] = mine[...]

    shape = (2 * half, extent)
    index = lax.broadcasted_iota(I32, shape, 0)
    place = lax.broadcasted_iota(I32, shape, 1) - extent // 2

    def row_factor(index, place):
        which = index // (2 * S)
        centre = jnp.full_like(index, off_ref[0, 0, 0, 0])
        plane = jnp.full_like(index, w_ref[0, 0, 0])
        for s in range(1, ns):
            centre = jnp.where(which == s, off_ref[0, 0, 0, s], centre)
            plane = jnp.where(which == s, w_ref[0, 0, s], plane)
        cell = centre + (index & (S - 1)) - S // 2
        bits = 2 * log_ext + 1
        quarter = ((index // S) & 1) << (bits - 2)
        return cos_of(phase_of(cell, place, plane, log_ext) + quarter, bits).astype(BF)

    eu[...] = row_factor(index, place)
    shape = (extent, 2 * half)
    eu_t[...] = row_factor(
        lax.broadcasted_iota(I32, shape, 1), lax.broadcasted_iota(I32, shape, 0) - extent // 2
    )

    step = min(512, nv)

    def kernels(i, carry):
        cut = pl.ds(pl.multiple_of(i * step, step), step)
        cells = lax.broadcasted_iota(I32, (S, step), 0).astype(F32)

        def table(position):
            d = position - cells
            return jnp.exp(d * d * (-0.5 / (KERNEL_WIDTH * KERNEL_WIDTH))).astype(BF).astype(F32)

        ku[:, cut] = table(uv_ref[0, 0, 0:1, cut])
        kv_all = table(uv_ref[0, 0, 1:2, cut])
        sub = sub_ref[0, :, cut]
        for s in range(ns):
            kv[s * S : (s + 1) * S, cut] = jnp.where(sub == s, kv_all, 0.0).astype(BF)
        return carry

    lax.fori_loop(0, nv // step, kernels, 0)

    fwd_copy.wait()
    spot = lax.broadcasted_iota(I32, (qs, lanes), 0) * lanes + (
        lax.broadcasted_iota(I32, (qs, lanes), 1) - fs // 2
    )
    low = lax.broadcasted_iota(I32, (rt, half), 1) < S
    bits = 2 * log_fs + 1

    def forward(i, carry):
        for u in range(batch):
            k = i * batch + u
            j = other(k)

            def hear():
                fact_copy(j, j).wait_recv()

            if u == 0:
                pl.when(i > 0)(hear)
            else:
                hear()
            told = facts[j].astype(I32)
            for s in range(ns):
                centre = jnp.broadcast_to(told[:, s : s + 1], (qs, lanes))
                plane = jnp.broadcast_to(told[:, ns + s : ns + s + 1], (qs, lanes))
                phase = phase_of(centre, spot, plane, log_fs)
                top = (u * ns + s) * rt
                for c in range(2):
                    ramp = cos_of(phase + (c << (bits - 2)), bits)
                    ramps[j, s, c] = ramp
                    for q in range(qs):
                        cut = slice(q * lanes, (q + 1) * lanes)
                        at = c * fs + q * lanes
                        xbuf[top : top + rt, at : at + lanes] = (
                            weighted[:, cut] * ramp[q : q + 1, :]
                        ).astype(BF)
        proj = jnp.dot(xbuf[...], t_fwd[...], preferred_element_type=F32)
        for u in range(batch):
            j = other(i * batch + u)
            first = proj[u * ns * rt : u * ns * rt + rt]
            second = proj[u * ns * rt + rt : u * ns * rt + 2 * rt]
            real = jnp.where(low, first, pltpu.roll(second, S, 1))
            imag = jnp.where(low, pltpu.roll(first, S, 1), second)
            sends[j, :, :half] = real.astype(BF)
            sends[j, :, half:] = imag.astype(BF)

            def go():
                msg_copy(j, me).start()

            if u == 0:
                pl.when(i > 0)(go)
            else:
                go()
        return carry

    lax.fori_loop(0, n // batch, forward, 0)
    got[me] = sends[me]

    def arrive(k, carry):
        j = other(k)
        msg_copy(j, j).wait_recv()
        return carry

    lax.fori_loop(1, n, arrive, 0)

    for p in range(n // 2):
        one = got[2 * p].astype(F32)
        two = got[2 * p + 1].astype(F32)
        for t in range(tay):
            cut = slice(t * rows, (t + 1) * rows)
            both = jnp.concatenate([one[cut], two[cut]], axis=0).astype(BF)
            stage[t, 2 * rows * p : 2 * rows * (p + 1), :] = both
    first_sub = lax.broadcasted_iota(I32, (S, half), 1) < S
    for t in range(tay):
        prod = jnp.dot(eu[...], stage[t], preferred_element_type=F32)
        re, im = [], []
        for s in range(ns):
            top = prod[2 * s * S : (2 * s + 1) * S]
            bot = prod[(2 * s + 1) * S : (2 * s + 2) * S]
            re.append(top[:, :half] - bot[:, half:])
            im.append(top[:, half:] + bot[:, :half])
        grid[2 * t * S : (2 * t + 1) * S, :] = jnp.where(first_sub, re[0], re[1]).astype(BF)
        grid[(2 * t + 1) * S : (2 * t + 2) * S, :] = jnp.where(first_sub, im[0], im[1]).astype(BF)

    gridded[...] = jnp.zeros_like(gridded)

    def visit(i, carry):
        cut = pl.ds(pl.multiple_of(i * step, step), step)
        ku_cut = ku[:, cut]
        kv_cut = kv[:, cut]
        spec = spec_ref[0, :, cut]
        powers = [jnp.ones_like(spec)]
        for t in range(1, tay):
            powers.append(powers[-1] * spec)
        cell = jnp.dot(grid[...], kv_cut, preferred_element_type=F32)
        number = lax.broadcasted_iota(I32, (1, step), 1) + i * step
        live = (number < counts_ref[0, 0]).astype(F32)
        spread = []
        left = []
        for c in range(2):
            predicted = jnp.zeros((1, step), F32)
            for t in range(tay):
                top = (2 * t + c) * S
                part = jnp.sum(cell[top : top + S] * ku_cut, axis=0, keepdims=True)
                predicted = predicted + part * powers[t]
            left.append(live * (obs_ref[0, 0, c : c + 1, cut] - predicted))
            res_ref[0, 0, c : c + 1, cut] = left[c]
        for t in range(tay):
            for c in range(2):
                spread.append(((left[c] * powers[t]) * ku_cut).astype(BF))
        spread = jnp.concatenate(spread, axis=0)
        gridded[...] += lax.dot_general(
            spread, kv_cut, (((1,), (1,)), ((), ())), preferred_element_type=F32
        )
        return carry

    lax.fori_loop(0, nv // step, visit, 0)

    def sent(k, carry):
        msg_copy(other(k), me).wait_send()
        return carry

    lax.fori_loop(1, n, sent, 0)
    for t in range(tay):
        re = gridded[2 * t * S : (2 * t + 1) * S, :].astype(BF).astype(F32)
        im = gridded[(2 * t + 1) * S : (2 * t + 2) * S, :].astype(BF).astype(F32)
        rhs = []
        for s in range(ns):
            keep = first_sub if s == 0 else jnp.logical_not(first_sub)
            re_s = jnp.where(keep, re, 0.0)
            im_s = jnp.where(keep, im, 0.0)
            rhs.append(jnp.concatenate([re_s, im_s], axis=1))
            rhs.append(jnp.concatenate([im_s, -re_s], axis=1))
        rhs = jnp.concatenate(rhs, axis=0).astype(BF)
        h[t] = jnp.dot(eu_t[...], rhs, preferred_element_type=F32)
    for j in range(n):
        sends[j] = jnp.concatenate(
            [h[t, j * rows : (j + 1) * rows, :] for t in range(tay)], axis=0
        ).astype(BF)

    def give(k, carry):
        back_copy(other(k), me).start()
        return carry

    lax.fori_loop(1, n, give, 0)
    back[me] = sends[me]
    bwd_copy.wait()

    weighted[...] = jnp.zeros_like(weighted)

    def collect(i, carry):
        for u in range(batch):
            j = other(i * batch + u)

            def hear():
                back_copy(j, j).wait_recv()

            if u == 0:
                pl.when(i > 0)(hear)
            else:
                hear()
        lhs = jnp.concatenate([back[other(i * batch + u)] for u in range(batch)], axis=0)

        def columns(q, carry):
            wide = 2 * ns * lanes
            z = jnp.dot(lhs, t_bwd[q], preferred_element_type=F32)
            at = pl.ds(pl.multiple_of(q * lanes, lanes), lanes)
            acc = weighted[:, at]
            for u in range(batch):
                j = other(i * batch + u)
                for s in range(ns):
                    for c in range(2):
                        v = (s * 2 + c) * lanes
                        ramp = ramps[j, s, c, pl.ds(q, 1), :]
                        acc = acc + z[u * rt : (u + 1) * rt, v : v + lanes] * ramp
            weighted[:, at] = acc
            return carry

        lax.fori_loop(0, qs, columns, 0)
        return carry

    lax.fori_loop(0, n // batch, collect, 0)

    norm_scale = 1.0 / (S * math.sqrt(groups * n * ns))
    scaled = gain * norm_scale
    per = groups // tay
    for f in range(groups):
        t = f // per
        cut = slice((f % per) * width, (f % per + 1) * width)
        image[f] = weighted[t * rows : (t + 1) * rows, cut] * scaled[:, cut]

    def peer(d):
        return lax.rem(group + d, groups)

    def share(d, carry):
        sum_copy(peer(d), group).start()
        return carry

    lax.fori_loop(1, groups, share, 0)
    total[...] = image[group]

    def add(d, carry):
        j = peer(d)
        sum_copy(j, j).wait_recv()
        total[...] += parts[j]
        return carry

    lax.fori_loop(1, groups, add, 0)

    def publish(d, carry):
        out_copy(peer(d), group).start()
        return carry

    lax.fori_loop(1, groups, publish, 0)
    dirty_ref[:, pl.ds(pl.multiple_of(group * width, lanes), width)] = total[...]

    def finish(k, carry):
        to = other(k)
        fact_copy(to, me).wait_send()
        back_copy(to, me).wait_send()
        return carry

    lax.fori_loop(1, n, finish, 0)

    def close(d, carry):
        j = peer(d)
        sum_copy(j, group).wait_send()
        out_copy(j, group).wait_send()
        out_copy(j, j).wait_recv()
        return carry

    lax.fori_loop(1, groups, close, 0)


def shards(model, beam, vis_obs, vis_uv, spectral, vis_subgrid, counts, uv_offsets, w_planes):
    rows = model.shape[0]
    fs = beam.shape[-1]
    tay = model.shape[1] // fs
    n = lax.axis_size("vis")
    groups = lax.axis_size("freq")
    extent = rows * n
    ns = w_planes.shape[-1]
    nv = vis_obs.shape[-1]
    rt = tay * rows
    width = 2 * ns * S
    lanes = 128
    qs = fs // lanes

    t_re, t_im = dft_tables(fs)
    fwd = np.concatenate(
        [np.concatenate([t_re.T, t_im.T], 1), np.concatenate([-t_im.T, t_re.T], 1)], 0
    )
    bwd = np.zeros((2, ns, S, qs, ns, 2, lanes), np.float32)
    for s in range(ns):
        split = (S, qs, lanes)
        bwd[0, s, :, :, s, 0] = t_re.reshape(split)
        bwd[1, s, :, :, s, 0] = t_im.reshape(split)
        bwd[0, s, :, :, s, 1] = -t_im.reshape(split)
        bwd[1, s, :, :, s, 1] = t_re.reshape(split)
    bwd = bwd.reshape(width, qs, ns * 2 * lanes).transpose(1, 0, 2)

    dma = pltpu.SemaphoreType.DMA
    vmem = pl.BlockSpec(memory_space=pltpu.VMEM)
    smem = pl.BlockSpec(memory_space=pltpu.SMEM)
    hbm = pl.BlockSpec(memory_space=pl.ANY)
    dims = (n, groups, tay, rows, fs, ns, nv)
    return pl.pallas_call(
        functools.partial(whole_kernel, dims),
        name="whole",
        out_shape=(
            jax.ShapeDtypeStruct((1, 1, 2, nv), F32),
            jax.ShapeDtypeStruct((rows, tay * fs), F32),
        ),
        in_specs=[vmem] * 6 + [smem] * 3 + [hbm] * 2,
        out_specs=(vmem, vmem),
        scratch_shapes=[
            pltpu.VMEM((2 * fs, 2 * S), BF),
            pltpu.VMEM((qs, width, ns * 2 * lanes), BF),
            pltpu.VMEM((1, lanes), F32),
            pltpu.VMEM((n, 1, lanes), F32),
            pltpu.VMEM((n, ns, 2, qs, lanes), F32),
            pltpu.VMEM((rt, fs), F32),
            pltpu.VMEM((8 * ns * rt, 2 * fs), BF),
            pltpu.VMEM((n, rt, width), BF),
            pltpu.VMEM((n, rt, width), BF),
            pltpu.VMEM((tay, extent, width), BF),
            pltpu.VMEM((width, extent), BF),
            pltpu.VMEM((extent, width), BF),
            pltpu.VMEM((S, nv), F32),
            pltpu.VMEM((ns * S, nv), BF),
            pltpu.VMEM((2 * tay * S, ns * S), BF),
            pltpu.VMEM((2 * tay * S, ns * S), F32),
            pltpu.VMEM((tay, extent, width), F32),
            pltpu.VMEM((n, rt, width), BF),
            pltpu.VMEM((groups, rows, tay * fs // groups), F32),
            pltpu.VMEM((groups, rows, tay * fs // groups), F32),
            pltpu.VMEM((rows, tay * fs // groups), F32),
            dma((2,)),
            dma((n,)), dma((n,)),
            dma((n,)), dma((n,)),
            dma((n,)), dma((n,)),
            dma((groups,)), dma((groups,)),
            dma((groups,)), dma((groups,)),
        ],
        compiler_params=pltpu.CompilerParams(
            collective_id=0, has_side_effects=True, vmem_limit_bytes=48 * 2**20
        ),
    )(
        model, beam, vis_obs, vis_uv, spectral, vis_subgrid, counts, uv_offsets, w_planes,
        jnp.asarray(fwd, BF), jnp.asarray(bwd, BF),
    )


def solution(mesh):
    in_specs = (
        P("vis", None),
        P("freq", "vis", None),
        P("freq", "vis", None, None),
        P("freq", "vis", None, None),
        P("freq", "vis", None),
        P("freq", "vis", None),
        P("freq", "vis"),
        P("freq", "vis", None, None),
        P("freq", "vis", None),
    )
    out_specs = (P("freq", "vis", None, None), P("vis", None))
    return jax.shard_map(shards, mesh=mesh, in_specs=in_specs, out_specs=out_specs, check_vma=False)
```

time: 703 us -> 105 us (0.15)
  waiting for transfers between devices: 587 us -> 0 us
  Pallas kernels: 0 us -> 93 us
  local copies, waits for them, and re-layouts: 58.4 us -> 9.61 us
  other arithmetic: 24.9 us -> 0 us
  matrix products: 16.4 us -> 0 us
  between operations: 15 us -> 1.3 us
    psum x2 -> x0, waiting for transfers between devices: 457 us -> none  [the longest x1 310 us: shards(): lax.psum(lax.dot_general(tables, section_stack, (((0,), (0,)), ((), ())),...]
    all_gather x1 -> x0, waiting for transfers between devices: 130 us -> none  [shards(): shard_rows = lax.all_gather(weighted, 'vis', axis=0, tiled=True)]
    pallas_call x0 -> x1, Pallas kernels: none -> 93 us  [shards(): pl.pallas_call(functools.partial(whole_kernel, dims), name='whole', out_s...]
    slice x6 -> x0, local copies, waits for them, and re-layouts: 22.6 us -> none  [the longest x2 17.4 us: shards(): side_prod[0, :, :, 0] + side_prod[1, :, :, 1]]
    reshape x4 -> x0, local copies, waits for them, and re-layouts: 17.8 us -> none  [the longest x2 13.3 us: shards(): side_prod = jnp.dot(cell_sum, ev_cols[sub_index], preferred_element_type=...]
    dot_general x8 -> x0, matrix products: 16.4 us -> none  [the longest x2 6.91 us: shards(): jnp.dot(cell_sum, ev_cols[sub_index], preferred_element_type=jnp.float32)]
    convert_element_type x4 -> x0, local copies, waits for them, and re-layouts: 11.1 us -> none  [shards(): (residual[:, None, None, :] * ku_all[sub_index]).astype(jnp.bfloat16)]
    convert_element_type x8 -> x0, other arithmetic: 8.67 us -> none  [the longest x2 2.93 us: axis_table(): jnp.cos(phases).astype(jnp.bfloat16)]
  transfers between devices with their start and end apart: 3 -> 0, of which waited for: 3 -> 0; matrix products, arithmetic and copies ran while one was open for 3% -> 0% of each run, Pallas kernels for 0% -> 0%
where the time goes in v2:
time: 105 us; the launch traced here: 104 us
  Pallas kernels  93 us (89%)
  local copies, waits for them, and re-layouts  9.61 us (9%)
  between operations  1.3 us (1%)
    pallas_call x1, Pallas kernels, shards(): pl.pallas_call(functools.partial(whole_kernel, dims), name='whole', out_s...  93 us
    unnamed x22, local copies, waits for them, and re-layouts  9.61 us

profile of v2, /device:TPU:1, one launch (start us, length us, event | category | flops | bytes accessed | tf_op | source)
XLA Modules:
  0.0 103.9 jit_solution(148428258805627939)
XLA Ops:
  1.3 0.0 copy-start
  1.3 1.6 %copy-done = bf16[8,256,512]{2,1,0:T(8,128)(2,1)S(1)} copy-done((bf16[8,256,512]{2,1,0:T(8,128)(2,1)S(1)}, bf16[8,256,512]{2,1,0:T(8,128)(2,1)}, u32[]{:S(2)}) %copy-start) | copy-done | bytes 2097176
  2.9 0.0 copy-start.1
  2.9 1.0 %copy-done.1 = bf16[2048,128]{1,0:T(8,128)(2,1)S(1)} copy-done((bf16[2048,128]{1,0:T(8,128)(2,1)S(1)}, bf16[2048,128]{1,0:T(8,128)(2,1)}, u32[]{:S(2)}) %copy-start.1) | copy-done | bytes 524312
  3.9 0.0 copy-start.2
  3.9 0.8 copy-done.2
  4.8 0.0 copy-start.3
  4.8 0.7 copy-done.3
  5.5 0.0 copy-start.4
  5.5 0.7 copy-done.4
  6.2 0.0 copy-start.5
  6.2 0.7 copy-done.5
  6.9 0.0 copy-start.6
  6.9 0.7 copy-done.6
  7.6 0.0 copy-start.7
  7.6 0.7 copy-done.7
  8.3 0.0 copy-start.8
  8.3 0.7 copy-done.8
  9.0 0.0 copy-start.9
  9.0 0.7 copy-done.9
  9.6 93.0 %whole.1 = (f32[1,1,2,2048]{3,2,1,0:T(2,128)S(1)}, f32[8,4096]{1,0:T(8,128)S(1)}) custom-call(bf16[8,4096]{1,0:T(8,128)(2,1)S(1)} %copy-done.2, bf16[1,8,1024]{2,1,0:T(8,128)(2,1)S(1)} %copy-done.3, f32[1,1,2,2048]{3,2,1,0:T(2,128)S(1)} %copy-done.4, f32[1,1,2,2048]{3,2,1,0:T(2,128)S(1)} %copy-done.5, f32[1,1,2048]{2,1,0:T(1,128)S(1)} %copy-done.6, ...), custom_call_target="tpu_custom_call" | custom-call | tf_op jit(solution)/shard_map/whole/pallas_call | solution.py:442
  102.7 0.6 copy.16
  103.3 0.7 copy.17
Async XLA Ops:
  1.3 1.6 %copy-start = (bf16[8,256,512]{2,1,0:T(8,128)(2,1)S(1)}, bf16[8,256,512]{2,1,0:T(8,128)(2,1)}, u32[]{:S(2)}) copy-start(bf16[8,256,512]{2,1,0:T(8,128)(2,1)} %constant.5.clone.bwd_hbm) | copy-start | bytes 6291460
  2.9 1.0 %copy-start.1 = (bf16[2048,128]{1,0:T(8,128)(2,1)S(1)}, bf16[2048,128]{1,0:T(8,128)(2,1)}, u32[]{:S(2)}) copy-start(bf16[2048,128]{1,0:T(8,128)(2,1)} %constant.4.clone.fwd_hbm) | copy-start | bytes 1572868
  3.9 0.8 copy-start.2
  4.8 0.7 copy-start.3
  5.5 0.7 copy-start.4
  6.2 0.7 copy-start.5
  6.9 0.7 copy-start.6
  7.6 0.7 copy-start.7
  8.3 0.7 copy-start.8
  9.0 0.7 copy-start.9

commit v3 on v2

v3 whole, which is shorter than its diff:
```python
import functools
import math

import jax
import jax.numpy as jnp
import numpy as np
from jax import lax
from jax.experimental import pallas as pl
from jax.experimental.pallas import tpu as pltpu
from jax.sharding import PartitionSpec as P

S = 64
KERNEL_WIDTH = 0.5
MESH = pl.DeviceIdType.MESH
BF = jnp.bfloat16
F32 = jnp.float32
I32 = jnp.int32


def dft_tables(pixels):
    cells = np.arange(S) - S // 2
    places = np.arange(pixels) - pixels // 2
    angle = -2.0 * np.pi * np.mod(cells[:, None] * places[None, :], pixels) / pixels
    return np.cos(angle).astype(np.float32), np.sin(angle).astype(np.float32)


def cos_of(phase, bits):
    full = 1 << bits
    phase = phase & (full - 1)
    phase = jnp.where(phase >= full // 2, full - phase, phase)
    x = (0.25 - phase.astype(F32) * (1.0 / full)) * (2.0 * math.pi)
    y = x * x
    total = jnp.full_like(x, -1.0 / math.factorial(11))
    for power in (9, 7, 5, 3, 1):
        sign = 1.0 if power % 4 == 1 else -1.0
        total = total * y + sign / math.factorial(power)
    return total * x


def phase_of(cell, place, w_plane, log2):
    pixels = 1 << log2
    linear = (cell * place) & (pixels - 1)
    quadratic = (w_plane * place * place) & (2 * pixels * pixels - 1)
    return (linear << (log2 + 1)) + quadratic


def offset(k):
    return ((k + 1) // 2) * (1 - 2 * ((k + 1) % 2))


def whole_kernel(
    dims,
    model_hbm, beam_hbm, obs_hbm, uv_hbm, spec_hbm, sub_hbm, counts_hbm, off_hbm, w_hbm,
    fwd_hbm, bwd_hbm,
    res_ref, dirty_ref,
    model_ref, beam_ref, obs_ref, uv_ref, spec_ref, sub_ref, counts_ref, off_ref, w_ref,
    t_fwd, t_bwd, mine, facts, ramps, packed, far_packed, beams, far_beams, weighted,
    xbuf, sends, got, stage, eu, eu_t, ku, kv, grid, gridded, h, back_sends, back, image, parts,
    total, far_total,
    tab_sem, fact_s, fact_r, pair_s, pair_r, msg_s, msg_r, back_s, back_r, sum_s, sum_r,
    out_s, out_r,
):
    n, groups, tay, rows, fs, ns, nv = dims
    rt = tay * rows
    extent = n * rows
    log_fs = fs.bit_length() - 1
    log_ext = extent.bit_length() - 1
    lanes = 128
    wide = 2 * S
    qs = fs // lanes
    batch = 8
    me = lax.axis_index("vis")
    group = lax.axis_index("freq")

    near = n // 2
    twin = lax.rem(me + near, n)

    def other(k):
        return lax.rem(me + offset(k) + n, n)

    def actor(k):
        return lax.rem(me - offset(k) + n, n)

    def twin_of(device):
        return lax.rem(device + near, n)

    def remote(src, dst, send, recv, axis, to):
        return pltpu.make_async_remote_copy(
            src_ref=src, dst_ref=dst, send_sem=send, recv_sem=recv,
            device_id={axis: to}, device_id_type=MESH,
        )

    def fact_copy(to, slot):
        return remote(mine, facts.at[slot], fact_s.at[to], fact_r.at[slot], "vis", to)

    def pair_copy(src, dst, index):
        return remote(src, dst, pair_s.at[index], pair_r.at[index], "vis", twin)

    def msg_copy(s, r, to, slot):
        return remote(
            sends.at[s, r, to], got.at[s, slot], msg_s.at[s, r, to], msg_r.at[s, slot], "vis", to
        )

    def back_copy(s, r, to, rows_of, slot):
        return remote(
            back_sends.at[s, rows_of], back.at[s, r, slot],
            back_s.at[s, rows_of], back_r.at[s, r, slot], "vis", to,
        )

    def sum_copy(r, to, slot):
        return remote(
            image.at[r, to], parts.at[r, slot], sum_s.at[r, to], sum_r.at[r, slot], "freq", to
        )

    width = tay * fs // groups

    def out_copy(to, slot):
        place = dirty_ref.at[:, pl.ds(pl.multiple_of(slot * width, lanes), width)]
        return remote(total.at[0], place, out_s.at[to], out_r.at[slot], "freq", to)

    loads = [
        (off_hbm, off_ref),
        (w_hbm, w_ref),
        (beam_hbm, beam_ref),
        (model_hbm, model_ref),
        (uv_hbm, uv_ref),
        (sub_hbm, sub_ref),
        (fwd_hbm, t_fwd),
        (counts_hbm, counts_ref),
        (spec_hbm, spec_ref),
        (obs_hbm, obs_ref),
        (bwd_hbm, t_bwd),
    ]
    loads = [pltpu.make_async_copy(a, b, tab_sem.at[i]) for i, (a, b) in enumerate(loads)]
    for load in loads:
        load.start()
    barrier = pltpu.get_barrier_semaphore()

    def greet(axis, to):
        pl.semaphore_signal(barrier, inc=1, device_id={axis: to}, device_id_type=MESH)

    greet("vis", twin)
    greet("vis", actor(near - 1))

    def greet_near(k, carry):
        greet("vis", other(near - k))
        return carry

    def greet_group(d, carry):
        greet("freq", lax.rem(group + d, groups))
        return carry

    lax.fori_loop(1, near, greet_near, 0)
    lax.fori_loop(1, groups, greet_group, 0)

    for load in loads[:4]:
        load.wait()
    lane = lax.broadcasted_iota(I32, (1, lanes), 1)
    fact = jnp.zeros((1, lanes), F32)
    for s in range(ns):
        fact = jnp.where(lane == s, off_ref[0, 0, 1, s].astype(F32), fact)
        fact = jnp.where(lane == ns + s, w_ref[0, 0, s].astype(F32), fact)
    mine[...] = fact
    gain = beam_ref[0].astype(F32)
    for t in range(tay):
        piece = (model_ref[:, t * fs : (t + 1) * fs].astype(F32) * gain).astype(BF)
        weighted[0, t * rows : (t + 1) * rows, :] = piece.astype(F32)
    packed[...] = weighted[0].astype(BF)
    beams[...] = jnp.concatenate([gain[:, : fs // 2], gain[:, fs // 2 :]], axis=0).astype(BF)

    pl.semaphore_wait(barrier, near + 1 + groups - 1)
    pair_copy(packed, far_packed, 0).start()

    def tell(k, carry):
        fact_copy(actor(k), me).start()
        return carry

    lax.fori_loop(1, near, tell, 0)
    pair_copy(beams, far_beams, 1).start()
    facts[me] = mine[...]

    loads[6].wait()
    spot = lax.broadcasted_iota(I32, (qs, lanes), 0) * lanes + (
        lax.broadcasted_iota(I32, (qs, lanes), 1) - fs // 2
    )
    bits = 2 * log_fs + 1

    def forward(r, s, i, carry):
        for u in range(batch):
            j = other(i * batch + u)

            def hear():
                fact_copy(j, j).wait_recv()

            if r == 0 and s == 0:
                if u == 0:
                    pl.when(i > 0)(hear)
                else:
                    hear()
            if r == 0:
                told = facts[j].astype(I32)
                centre = jnp.broadcast_to(told[:, s : s + 1], (qs, lanes))
                plane = jnp.broadcast_to(told[:, ns + s : ns + s + 1], (qs, lanes))
                phase = phase_of(centre, spot, plane, log_fs)
                for c in range(2):
                    ramps[j, s, c] = cos_of(phase + (c << (bits - 2)), bits)
            for c in range(2):
                ramp = ramps[j, s, c]
                for q in range(qs):
                    cut = slice(q * lanes, (q + 1) * lanes)
                    at = c * fs + q * lanes
                    xbuf[u * rt : (u + 1) * rt, at : at + lanes] = (
                        weighted[r, :, cut] * ramp[q : q + 1, :]
                    ).astype(BF)
        proj = jnp.dot(xbuf[...], t_fwd[...], preferred_element_type=F32).astype(BF)
        for u in range(batch):
            j = other(i * batch + u)
            sends[s, r, j] = proj[u * rt : (u + 1) * rt]

            def go():
                msg_copy(s, r, j, me if r == 0 else twin).start()

            if u == 0:
                pl.when(i > 0)(go)
            else:
                go()
        return carry

    for r in range(2):
        if r == 1:
            pair_copy(packed, far_packed, 0).wait_recv()
            weighted[1] = far_packed[...].astype(F32)
        for s in range(ns):
            lax.fori_loop(0, near // batch, functools.partial(forward, r, s), 0)
            got[s, me if r == 0 else twin] = sends[s, r, me]
        if r == 0:
            def row_factor(s, index, place):
                cell = off_ref[0, 0, 0, s] + (index & (S - 1)) - S // 2
                bits = 2 * log_ext + 1
                quarter = (index // S) << (bits - 2)
                return cos_of(phase_of(cell, place, w_ref[0, 0, s], log_ext) + quarter, bits).astype(BF)

            def place_of(shape, axis):
                return lax.broadcasted_iota(I32, shape, axis) - extent // 2

            shape = (wide, extent)
            turned = (extent, wide)
            for s in range(ns):
                eu[s] = row_factor(s, lax.broadcasted_iota(I32, shape, 0), place_of(shape, 1))
                eu_t[s] = row_factor(s, lax.broadcasted_iota(I32, turned, 1), place_of(turned, 0))

            loads[4].wait()
            loads[5].wait()
            step = min(512, nv)

            def kernels(i, carry):
                cut = pl.ds(pl.multiple_of(i * step, step), step)
                cells = lax.broadcasted_iota(I32, (S, step), 0).astype(F32)

                def table(position):
                    d = position - cells
                    return jnp.exp(d * d * (-0.5 / (KERNEL_WIDTH * KERNEL_WIDTH))).astype(BF).astype(F32)

                ku[:, cut] = table(uv_ref[0, 0, 0:1, cut])
                kv_all = table(uv_ref[0, 0, 1:2, cut])
                sub = sub_ref[0, :, cut]
                for s in range(ns):
                    masked = jnp.where(sub == s, kv_all, 0.0).astype(BF)
                    kv[s, :S, cut] = masked
                    kv[s, S:, cut] = masked
                return carry

            lax.fori_loop(0, nv // step, kernels, 0)

    for load in loads[7:10]:
        load.wait()
    first = lax.broadcasted_iota(I32, (S, wide), 1) < S
    sign = jnp.where(first, -1.0, 1.0)

    for s in range(ns):

        def arrive(k, carry):
            j = actor(k)
            msg_copy(s, 0, j, j).wait_recv()
            msg_copy(s, 1, j, twin_of(j)).wait_recv()
            return carry

        lax.fori_loop(1, near, arrive, 0)

        for p in range(n // 2):
            one = got[s, 2 * p].astype(F32)
            two = got[s, 2 * p + 1].astype(F32)
            for t in range(tay):
                cut = slice(t * rows, (t + 1) * rows)
                both = jnp.concatenate([one[cut], two[cut]], axis=0).astype(BF)
                stage[t, 2 * rows * p : 2 * rows * (p + 1), :] = both
        for t in range(tay):
            prod = jnp.dot(eu[s], stage[t], preferred_element_type=F32)
            pair = prod[:S] + sign * pltpu.roll(prod[S:], S, 1)
            grid[2 * t * S : (2 * t + 1) * S, :] = jnp.where(first, pair, 0.0).astype(BF)
            grid[(2 * t + 1) * S : (2 * t + 2) * S, :] = jnp.where(first, 0.0, pair).astype(BF)

        gridded[...] = jnp.zeros_like(gridded)

        def visit(i, carry):
            cut = pl.ds(pl.multiple_of(i * step, step), step)
            ku_cut = ku[:, cut]
            kv_cut = kv[s, :, cut]
            spec = spec_ref[0, :, cut]
            powers = [jnp.ones_like(spec)]
            for t in range(1, tay):
                powers.append(powers[-1] * spec)
            cell = jnp.dot(grid[...], kv_cut, preferred_element_type=F32)
            number = lax.broadcasted_iota(I32, (1, step), 1) + i * step
            live = jnp.logical_and(number < counts_ref[0, 0], sub_ref[0, :, cut] == s)
            live = live.astype(F32)
            spread = []
            left = []
            for c in range(2):
                predicted = jnp.zeros((1, step), F32)
                for t in range(tay):
                    top = (2 * t + c) * S
                    part = jnp.sum(cell[top : top + S] * ku_cut, axis=0, keepdims=True)
                    predicted = predicted + part * powers[t]
                left.append(live * (obs_ref[0, 0, c : c + 1, cut] - predicted))
                if s == 0:
                    res_ref[0, 0, c : c + 1, cut] = left[c]
                else:
                    res_ref[0, 0, c : c + 1, cut] += left[c]
            for t in range(tay):
                for c in range(2):
                    spread.append(((left[c] * powers[t]) * ku_cut).astype(BF))
            spread = jnp.concatenate(spread, axis=0)
            gridded[...] += lax.dot_general(
                spread, kv_cut, (((1,), (1,)), ((), ())), preferred_element_type=F32
            )
            return carry

        lax.fori_loop(0, nv // step, visit, 0)

        for t in range(tay):
            re = gridded[2 * t * S : (2 * t + 1) * S, :]
            im = gridded[(2 * t + 1) * S : (2 * t + 2) * S, :]
            rhs = jnp.concatenate([jnp.where(first, re, im), jnp.where(first, im, -re)], axis=0)
            h[t] = jnp.dot(eu_t[s], rhs.astype(BF), preferred_element_type=F32)
        for j in range(n):
            back_sends[s, j] = jnp.concatenate(
                [h[t, j * rows : (j + 1) * rows, :] for t in range(tay)], axis=0
            ).astype(BF)

        for r in (1, 0):

            def give(k, carry):
                to = actor(k)
                back_copy(s, r, to, to if r == 0 else twin_of(to), me).start()
                return carry

            lax.fori_loop(1, near, give, 0)
        back[s, 0, me] = back_sends[s, me]
        back[s, 1, me] = back_sends[s, twin]

    loads[10].wait()
    weighted[...] = jnp.zeros_like(weighted)
    norm_scale = 1.0 / (S * math.sqrt(groups * n * ns))
    per = groups // tay
    pair_copy(beams, far_beams, 1).wait_recv()
    far_gain = far_beams[...].astype(F32)
    far_gain = jnp.concatenate([far_gain[:rows], far_gain[rows:]], axis=1)

    def peer(d):
        return lax.rem(group + d, groups)

    for s in range(ns):
        for r in (1, 0):

            def collect(i, carry):
                blocks = [other(i * batch + u) for u in range(batch)]
                for u, j in enumerate(blocks):

                    def hear():
                        back_copy(s, r, j, j, j).wait_recv()

                    if u == 0:
                        pl.when(i > 0)(hear)
                    else:
                        hear()
                lhs = jnp.concatenate([back[s, r, j] for j in blocks], axis=0)
                for q in range(qs):
                    z = jnp.dot(lhs, t_bwd[q], preferred_element_type=F32)
                    cut = slice(q * lanes, (q + 1) * lanes)
                    acc = weighted[r, :, cut]
                    for u, j in enumerate(blocks):
                        for c in range(2):
                            ramp = ramps[j, s, c, q : q + 1, :]
                            part = z[u * rt : (u + 1) * rt, c * lanes : (c + 1) * lanes]
                            acc = acc + part * ramp
                    weighted[r, :, cut] = acc
                return carry

            lax.fori_loop(0, near // batch, collect, 0)
            if s == ns - 1:
                scaled = (gain if r == 0 else far_gain) * norm_scale
                for f in range(groups):
                    t = f // per
                    cut = slice((f % per) * width, (f % per + 1) * width)
                    image[r, f] = weighted[r, t * rows : (t + 1) * rows, cut] * scaled[:, cut]

                def share(d, carry):
                    sum_copy(r, peer(d), group).start()
                    return carry

                lax.fori_loop(1, groups, share, 0)

    for r in (1, 0):
        total[r] = image[r, group]

        def add(d, carry):
            j = peer(d)
            sum_copy(r, j, j).wait_recv()
            total[r] += parts[r, j]
            return carry

        lax.fori_loop(1, groups, add, 0)
        if r == 1:
            pair_copy(total.at[1], far_total, 2).start()
    pair_copy(total.at[1], far_total, 2).wait_recv()
    total[0] += far_total[...]

    def publish(d, carry):
        out_copy(peer(d), group).start()
        return carry

    lax.fori_loop(1, groups, publish, 0)
    dirty_ref[:, pl.ds(pl.multiple_of(group * width, lanes), width)] = total[0]

    pair_copy(packed, far_packed, 0).wait_send()
    pair_copy(beams, far_beams, 1).wait_send()
    pair_copy(total.at[1], far_total, 2).wait_send()

    def finish(k, carry):
        to = other(k)
        of = actor(k)
        fact_copy(of, me).wait_send()
        for s in range(ns):
            for r in range(2):
                msg_copy(s, r, to, me).wait_send()
                back_copy(s, r, of, of if r == 0 else twin_of(of), me).wait_send()
        return carry

    lax.fori_loop(1, near, finish, 0)

    def close(d, carry):
        j = peer(d)
        for r in range(2):
            sum_copy(r, j, group).wait_send()
        out_copy(j, group).wait_send()
        out_copy(j, j).wait_recv()
        return carry

    lax.fori_loop(1, groups, close, 0)


def shards(model, beam, vis_obs, vis_uv, spectral, vis_subgrid, counts, uv_offsets, w_planes):
    rows = model.shape[0]
    fs = beam.shape[-1]
    tay = model.shape[1] // fs
    n = lax.axis_size("vis")
    groups = lax.axis_size("freq")
    extent = rows * n
    ns = w_planes.shape[-1]
    nv = vis_obs.shape[-1]
    rt = tay * rows
    wide = 2 * S
    lanes = 128
    qs = fs // lanes

    t_re, t_im = dft_tables(fs)
    fwd = np.concatenate(
        [np.concatenate([t_re.T, t_im.T], 1), np.concatenate([-t_im.T, t_re.T], 1)], 0
    )
    split = (S, qs, 1, lanes)
    re, im = t_re.reshape(split), t_im.reshape(split)
    bwd = np.concatenate(
        [np.concatenate([re, -im], 2), np.concatenate([im, re], 2)], 0
    )
    bwd = bwd.reshape(2 * S, qs, 2 * lanes).transpose(1, 0, 2)

    dma = pltpu.SemaphoreType.DMA
    vmem = pl.BlockSpec(memory_space=pltpu.VMEM)
    hbm = pl.BlockSpec(memory_space=pltpu.HBM)
    dims = (n, groups, tay, rows, fs, ns, nv)
    return pl.pallas_call(
        functools.partial(whole_kernel, dims),
        name="whole",
        out_shape=(
            jax.ShapeDtypeStruct((1, 1, 2, nv), F32),
            jax.ShapeDtypeStruct((rows, tay * fs), F32),
        ),
        in_specs=[hbm] * 11,
        out_specs=(vmem, vmem),
        scratch_shapes=[
            pltpu.VMEM((rows, tay * fs), BF),
            pltpu.VMEM((1, rows, fs), BF),
            pltpu.VMEM((1, 1, 2, nv), F32),
            pltpu.VMEM((1, 1, 2, nv), F32),
            pltpu.VMEM((1, 1, nv), F32),
            pltpu.VMEM((1, 1, nv), I32),
            pltpu.SMEM((1, 1), I32),
            pltpu.SMEM((1, 1, 2, ns), I32),
            pltpu.SMEM((1, 1, ns), I32),
            pltpu.VMEM((2 * fs, wide), BF),
            pltpu.VMEM((qs, wide, 2 * lanes), BF),
            pltpu.VMEM((1, lanes), F32),
            pltpu.VMEM((n, 1, lanes), F32),
            pltpu.VMEM((n, ns, 2, qs, lanes), F32),
            pltpu.VMEM((rt, fs), BF),
            pltpu.VMEM((rt, fs), BF),
            pltpu.VMEM((2 * rows, fs // 2), BF),
            pltpu.VMEM((2 * rows, fs // 2), BF),
            pltpu.VMEM((2, rt, fs), F32),
            pltpu.VMEM((8 * rt, 2 * fs), BF),
            pltpu.VMEM((ns, 2, n, rt, wide), BF),
            pltpu.VMEM((ns, n, rt, wide), BF),
            pltpu.VMEM((tay, extent, wide), BF),
            pltpu.VMEM((ns, wide, extent), BF),
            pltpu.VMEM((ns, extent, wide), BF),
            pltpu.VMEM((S, nv), F32),
            pltpu.VMEM((ns, wide, nv), BF),
            pltpu.VMEM((2 * tay * S, wide), BF),
            pltpu.VMEM((2 * tay * S, wide), F32),
            pltpu.VMEM((tay, extent, wide), F32),
            pltpu.VMEM((ns, n, rt, wide), BF),
            pltpu.VMEM((ns, 2, n, rt, wide), BF),
            pltpu.VMEM((2, groups, rows, tay * fs // groups), F32),
            pltpu.VMEM((2, groups, rows, tay * fs // groups), F32),
            pltpu.VMEM((2, rows, tay * fs // groups), F32),
            pltpu.VMEM((rows, tay * fs // groups), F32),
            dma((11,)),
            dma((n,)), dma((n,)),
            dma((3,)), dma((3,)),
            dma((ns, 2, n)), dma((ns, n)),
            dma((ns, n)), dma((ns, 2, n)),
            dma((2, groups)), dma((2, groups)),
            dma((groups,)), dma((groups,)),
        ],
        compiler_params=pltpu.CompilerParams(
            collective_id=0, has_side_effects=True, vmem_limit_bytes=60 * 2**20
        ),
    )(
        model, beam, vis_obs, vis_uv, spectral, vis_subgrid, counts, uv_offsets, w_planes,
        np.ascontiguousarray(fwd).astype(BF), np.ascontiguousarray(bwd).astype(BF),
    )


def solution(mesh):
    in_specs = (
        P("vis", None),
        P("freq", "vis", None),
        P("freq", "vis", None, None),
        P("freq", "vis", None, None),
        P("freq", "vis", None),
        P("freq", "vis", None),
        P("freq", "vis"),
        P("freq", "vis", None, None),
        P("freq", "vis", None),
    )
    out_specs = (P("freq", "vis", None, None), P("vis", None))
    return jax.shard_map(shards, mesh=mesh, in_specs=in_specs, out_specs=out_specs, check_vma=False)
```

time: 105 us -> 83.7 us (0.80)
  Pallas kernels: 93 us -> 79.3 us
  local copies, waits for them, and re-layouts: 9.61 us -> 2.89 us
    pallas_call x1, Pallas kernels: 93 us -> 79.3 us  [shards(): pl.pallas_call(functools.partial(whole_kernel, dims), name='whole', out_s...]
    unnamed x22 -> x2, local copies, waits for them, and re-layouts: 9.61 us -> 2.89 us
where the time goes in v3:
time: 83.7 us; the launch traced here: 83.5 us
  Pallas kernels  79.3 us (95%)
  local copies, waits for them, and re-layouts  2.89 us (3%)
  between operations  1.29 us (2%)
    pallas_call x1, Pallas kernels, shards(): pl.pallas_call(functools.partial(whole_kernel, dims), name='whole', out_s...  79.3 us
    unnamed x2, local copies, waits for them, and re-layouts  2.89 us

profile of v3, /device:TPU:1, one launch (start us, length us, event | category | flops | bytes accessed | tf_op | source)
XLA Modules:
  0.0 83.5 jit_solution(5653472770389841376)
XLA Ops:
  1.3 79.3 %whole.1 = (f32[1,1,2,2048]{3,2,1,0:T(2,128)}, f32[8,4096]{1,0:T(8,128)}) custom-call(bf16[8,4096]{1,0:T(8,128)(2,1)} %model_hbm.1, bf16[1,8,1024]{2,1,0:T(8,128)(2,1)} %beam_hbm.1, f32[1,1,2,2048]{3,2,1,0:T(2,128)} %obs_hbm.1, f32[1,1,2,2048]{3,2,1,0:T(2,128)} %uv_hbm.1, f32[1,1,2048]{2,1,0:T(1,128)} %spec_hbm.1, s32[1,1,2048]{2,1,0:T(1,128)} %sub_hbm.1, ...), custom_call_target="tpu_custom_call" | custom-call | tf_op jit(solution)/shard_map/whole/pallas_call | solution.py:492
  80.6 1.3 %copy.16 = f32[1,1,2,2048]{3,2,1,0:T(2,128)} copy(f32[1,1,2,2048]{3,2,1,0:T(2,128)} %get-tuple-element.4) | data formatting | bytes 32768
  82.0 1.6 %copy.17 = f32[8,4096]{1,0:T(8,128)} copy(f32[8,4096]{1,0:T(8,128)} %get-tuple-element.5) | data formatting | bytes 262144

commit v4 on v3

v4 whole, which is shorter than its diff:
```python
import functools
import math

import jax
import jax.numpy as jnp
import numpy as np
from jax import lax
from jax.experimental import pallas as pl
from jax.experimental.pallas import tpu as pltpu
from jax.sharding import PartitionSpec as P

S = 64
KERNEL_WIDTH = 0.5
MESH = pl.DeviceIdType.MESH
BF = jnp.bfloat16
F32 = jnp.float32
I32 = jnp.int32


def dft_tables(pixels):
    cells = np.arange(S) - S // 2
    places = np.arange(pixels) - pixels // 2
    angle = -2.0 * np.pi * np.mod(cells[:, None] * places[None, :], pixels) / pixels
    return np.cos(angle).astype(np.float32), np.sin(angle).astype(np.float32)


def cos_of(phase, bits):
    full = 1 << bits
    phase = phase & (full - 1)
    phase = jnp.where(phase >= full // 2, full - phase, phase)
    x = (0.25 - phase.astype(F32) * (1.0 / full)) * (2.0 * math.pi)
    y = x * x
    total = jnp.full_like(x, -1.0 / math.factorial(11))
    for power in (9, 7, 5, 3, 1):
        sign = 1.0 if power % 4 == 1 else -1.0
        total = total * y + sign / math.factorial(power)
    return total * x


def phase_of(cell, place, w_plane, log2):
    pixels = 1 << log2
    linear = (cell * place) & (pixels - 1)
    quadratic = (w_plane * place * place) & (2 * pixels * pixels - 1)
    return (linear << (log2 + 1)) + quadratic


def offset(k):
    return ((k + 1) // 2) * (1 - 2 * ((k + 1) % 2))


def whole_kernel(
    dims,
    model_hbm, beam_hbm, obs_hbm, uv_hbm, spec_hbm, sub_hbm, counts_hbm, off_hbm, w_hbm,
    fwd_hbm, bwd_hbm,
    res_ref, dirty_ref,
    model_ref, beam_ref, obs_ref, uv_ref, spec_ref, sub_ref, counts_ref, off_ref, w_ref,
    t_fwd, t_bwd, mine, facts, ramps, hold, beams, weighted,
    xbuf, sends, got, stage, eu, eu_t, ku, kv, grid, gridded, h, back_sends, back, image, parts,
    stage_f32, total, homes, result,
    tab_sem, fact_s, fact_r, pair_s, pair_r, beam_s, beam_r, home_s, home_r,
    msg_s, msg_r, back_s, back_r, sum_s, sum_r, out_s, out_r,
):
    n, groups, tay, rows, fs, ns, nv = dims
    rt = tay * rows
    extent = n * rows
    log_fs = fs.bit_length() - 1
    log_ext = extent.bit_length() - 1
    lanes = 128
    wide = 2 * S
    qs = fs // lanes
    me = lax.axis_index("vis")
    group = lax.axis_index("freq")

    sets = 4
    close = n // sets

    def other(k):
        return lax.rem(me + offset(k) + n, n)

    def actor(k):
        return lax.rem(me - offset(k) + n, n)

    def owner(device, e):
        return lax.rem(device + e * close, n)

    def helper(e):
        return lax.rem(me + n - e * close, n)

    def remote(src, dst, send, recv, axis, to):
        return pltpu.make_async_remote_copy(
            src_ref=src, dst_ref=dst, send_sem=send, recv_sem=recv,
            device_id={axis: to}, device_id_type=MESH,
        )

    def fact_copy(k, to, slot):
        return remote(mine, facts.at[slot], fact_s.at[k], fact_r.at[k], "vis", to)

    def pair_copy(e, part):
        cut = pl.ds(part * (rt // 2), rt // 2)
        return remote(
            hold.at[1 if e == 2 else 0, cut], hold.at[e, cut],
            pair_s.at[2 * e + part], pair_r.at[2 * e + part], "vis", helper(1 if e == 2 else e),
        )

    def beam_copy(e):
        return remote(
            beams.at[1 if e == 2 else 0], beams.at[e], beam_s.at[e], beam_r.at[e],
            "vis", helper(1 if e == 2 else e),
        )

    def home_copy(e):
        return remote(
            total.at[e], homes.at[e], home_s.at[e], home_r.at[e],
            "vis", owner(me, 1 if e == 2 else e),
        )

    def msg_copy(s, e, k, to, slot):
        return remote(
            sends.at[s, e, to], got.at[s, slot], msg_s.at[s, e, k], msg_r.at[s, e, k], "vis", to
        )

    def back_copy(s, e, k, to, rows_of, slot):
        return remote(
            back_sends.at[s, rows_of], back.at[s, e, slot],
            back_s.at[s, e, k], back_r.at[s, e, k], "vis", to,
        )

    tall = rows * tay * fs // groups // lanes

    def sum_copy(r, to, slot):
        which = pl.ds(tall, (sets - 1) * tall) if r else pl.ds(0, tall)
        return remote(
            image.at[to, which], parts.at[slot, which],
            sum_s.at[r, to], sum_r.at[r, slot], "freq", to,
        )

    width = tay * fs // groups

    def out_copy(to, slot):
        place = dirty_ref.at[:, pl.ds(pl.multiple_of(slot * width, lanes), width)]
        return remote(result, place, out_s.at[to], out_r.at[slot], "freq", to)

    loads = [
        (off_hbm, off_ref),
        (w_hbm, w_ref),
        (beam_hbm, beam_ref),
        (model_hbm, model_ref),
        (uv_hbm, uv_ref),
        (sub_hbm, sub_ref),
        (fwd_hbm, t_fwd),
        (counts_hbm, counts_ref),
        (spec_hbm, spec_ref),
        (obs_hbm, obs_ref),
        (bwd_hbm, t_bwd),
    ]
    loads = [pltpu.make_async_copy(a, b, tab_sem.at[i]) for i, (a, b) in enumerate(loads)]
    for load in loads:
        load.start()
    barrier = pltpu.get_barrier_semaphore()

    def greet(axis, to):
        pl.semaphore_signal(barrier, inc=1, device_id={axis: to}, device_id_type=MESH)

    greet("vis", helper(1))
    greet("vis", helper(3))
    greet("vis", actor(close - 1))

    def greet_near(k, carry):
        greet("vis", other(close - k))
        return carry

    def greet_group(d, carry):
        greet("freq", lax.rem(group + d, groups))
        return carry

    lax.fori_loop(1, close, greet_near, 0)
    lax.fori_loop(1, groups, greet_group, 0)

    for load in loads[:4]:
        load.wait()
    lane = lax.broadcasted_iota(I32, (1, lanes), 1)
    fact = jnp.zeros((1, lanes), F32)
    for s in range(ns):
        fact = jnp.where(lane == s, off_ref[0, 0, 1, s].astype(F32), fact)
        fact = jnp.where(lane == ns + s, w_ref[0, 0, s].astype(F32), fact)
    mine[...] = fact
    gain = beam_ref[0].astype(F32)
    for t in range(tay):
        piece = (model_ref[:, t * fs : (t + 1) * fs].astype(F32) * gain).astype(BF)
        weighted[0, t * rows : (t + 1) * rows, :] = piece.astype(F32)
    hold[0] = weighted[0].astype(BF)
    beams[0] = jnp.concatenate([gain[:, : fs // 2], gain[:, fs // 2 :]], axis=0).astype(BF)

    pl.semaphore_wait(barrier, close + 2 + groups - 1)
    for e in (1, 3):
        for part in range(2):
            pair_copy(e, part).start()

    def tell(k, carry):
        fact_copy(k, actor(k), me).start()
        return carry

    lax.fori_loop(1, close, tell, 0)
    for e in (1, 3):
        beam_copy(e).start()
    facts[me] = mine[...]

    loads[6].wait()
    spot = lax.broadcasted_iota(I32, (qs, lanes), 0) * lanes + (
        lax.broadcasted_iota(I32, (qs, lanes), 1) - fs // 2
    )
    bits = 2 * log_fs + 1

    blocks = [other(u) for u in range(close)]

    def forward(e, s, carry):
        for u, j in enumerate(blocks):
            if e == 0:
                if s == 0 and u > 0:
                    fact_copy(u, j, j).wait_recv()
                told = facts[j].astype(I32)
                centre = jnp.broadcast_to(told[:, s : s + 1], (qs, lanes))
                plane = jnp.broadcast_to(told[:, ns + s : ns + s + 1], (qs, lanes))
                phase = phase_of(centre, spot, plane, log_fs)
                for c in range(2):
                    ramps[j, s, c] = cos_of(phase + (c << (bits - 2)), bits)
            for c in range(2):
                ramp = ramps[j, s, c]
                for q in range(qs):
                    cut = slice(q * lanes, (q + 1) * lanes)
                    at = c * fs + q * lanes
                    xbuf[u * rt : (u + 1) * rt, at : at + lanes] = (
                        weighted[e, :, cut] * ramp[q : q + 1, :]
                    ).astype(BF)
        proj = jnp.dot(xbuf[...], t_fwd[...], preferred_element_type=F32).astype(BF)
        for u, j in enumerate(blocks):
            sends[s, e, j] = proj[u * rt : (u + 1) * rt]
            if u > 0:
                msg_copy(s, e, u, j, owner(me, e)).start()
        got[s, owner(me, e)] = sends[s, e, me]
        return carry

    for s in range(ns):
        forward(0, s, 0)

    def row_factor(s, index, place):
        cell = off_ref[0, 0, 0, s] + (index & (S - 1)) - S // 2
        bits = 2 * log_ext + 1
        quarter = (index // S) << (bits - 2)
        return cos_of(phase_of(cell, place, w_ref[0, 0, s], log_ext) + quarter, bits).astype(BF)

    def place_of(shape, axis):
        return lax.broadcasted_iota(I32, shape, axis) - extent // 2

    shape = (wide, extent)
    turned = (extent, wide)
    for s in range(ns):
        eu[s] = row_factor(s, lax.broadcasted_iota(I32, shape, 0), place_of(shape, 1))
        eu_t[s] = row_factor(s, lax.broadcasted_iota(I32, turned, 1), place_of(turned, 0))

    loads[4].wait()
    loads[5].wait()
    step = min(512, nv)

    def kernels(i, carry):
        cut = pl.ds(pl.multiple_of(i * step, step), step)
        cells = lax.broadcasted_iota(I32, (S, step), 0).astype(F32)

        def table(position):
            d = position - cells
            return jnp.exp(d * d * (-0.5 / (KERNEL_WIDTH * KERNEL_WIDTH))).astype(BF).astype(F32)

        ku[:, cut] = table(uv_ref[0, 0, 0:1, cut])
        kv_all = table(uv_ref[0, 0, 1:2, cut])
        sub = sub_ref[0, :, cut]
        for s in range(ns):
            masked = jnp.where(sub == s, kv_all, 0.0).astype(BF)
            kv[s, :S, cut] = masked
            kv[s, S:, cut] = masked
        return carry

    lax.fori_loop(0, nv // step, kernels, 0)

    for part in range(2):
        pair_copy(1, part).wait_recv()
        pair_copy(2, part).start()
    for e in (1, 3, 2):
        if e > 1:
            for part in range(2):
                pair_copy(e, part).wait_recv()
        weighted[e] = hold[e].astype(F32)
        lax.fori_loop(0, ns, functools.partial(forward, e), 0)
        if e == 1:
            beam_copy(1).wait_recv()
            beam_copy(2).start()

    for load in loads[7:10]:
        load.wait()
    first = lax.broadcasted_iota(I32, (S, wide), 1) < S
    sign = jnp.where(first, -1.0, 1.0)

    for s in range(ns):

        def arrive(k, carry):
            j = actor(k)
            for e in range(sets):
                msg_copy(s, e, k, j, owner(j, e)).wait_recv()
            return carry

        lax.fori_loop(1, close, arrive, 0)

        for p in range(n // 2):
            one = got[s, 2 * p].astype(F32)
            two = got[s, 2 * p + 1].astype(F32)
            for t in range(tay):
                cut = slice(t * rows, (t + 1) * rows)
                both = jnp.concatenate([one[cut], two[cut]], axis=0).astype(BF)
                stage[t, 2 * rows * p : 2 * rows * (p + 1), :] = both
        for t in range(tay):
            prod = jnp.dot(eu[s], stage[t], preferred_element_type=F32)
            pair = prod[:S] + sign * pltpu.roll(prod[S:], S, 1)
            grid[2 * t * S : (2 * t + 1) * S, :] = jnp.where(first, pair, 0.0).astype(BF)
            grid[(2 * t + 1) * S : (2 * t + 2) * S, :] = jnp.where(first, 0.0, pair).astype(BF)

        gridded[...] = jnp.zeros_like(gridded)

        def visit(i, carry):
            cut = pl.ds(pl.multiple_of(i * step, step), step)
            ku_cut = ku[:, cut]
            kv_cut = kv[s, :, cut]
            spec = spec_ref[0, :, cut]
            powers = [jnp.ones_like(spec)]
            for t in range(1, tay):
                powers.append(powers[-1] * spec)
            cell = jnp.dot(grid[...], kv_cut, preferred_element_type=F32)
            number = lax.broadcasted_iota(I32, (1, step), 1) + i * step
            live = jnp.logical_and(number < counts_ref[0, 0], sub_ref[0, :, cut] == s)
            live = live.astype(F32)
            spread = []
            left = []
            for c in range(2):
                predicted = jnp.zeros((1, step), F32)
                for t in range(tay):
                    top = (2 * t + c) * S
                    part = jnp.sum(cell[top : top + S] * ku_cut, axis=0, keepdims=True)
                    predicted = predicted + part * powers[t]
                left.append(live * (obs_ref[0, 0, c : c + 1, cut] - predicted))
                if s == 0:
                    res_ref[0, 0, c : c + 1, cut] = left[c]
                else:
                    res_ref[0, 0, c : c + 1, cut] += left[c]
            for t in range(tay):
                for c in range(2):
                    spread.append(((left[c] * powers[t]) * ku_cut).astype(BF))
            spread = jnp.concatenate(spread, axis=0)
            gridded[...] += lax.dot_general(
                spread, kv_cut, (((1,), (1,)), ((), ())), preferred_element_type=F32
            )
            return carry

        lax.fori_loop(0, nv // step, visit, 0, unroll=True)

        for t in range(tay):
            re = gridded[2 * t * S : (2 * t + 1) * S, :]
            im = gridded[(2 * t + 1) * S : (2 * t + 2) * S, :]
            rhs = jnp.concatenate([jnp.where(first, re, im), jnp.where(first, im, -re)], axis=0)
            h[t] = jnp.dot(eu_t[s], rhs.astype(BF), preferred_element_type=F32)
        for j in range(n):
            back_sends[s, j] = jnp.concatenate(
                [h[t, j * rows : (j + 1) * rows, :] for t in range(tay)], axis=0
            ).astype(BF)

        for e in (2, 1, 3, 0):

            def give(k, carry):
                to = actor(k)
                back_copy(s, e, k, to, owner(to, e), me).start()
                return carry

            lax.fori_loop(1, close, give, 0)
        for e in range(sets):
            back[s, e, me] = back_sends[s, owner(me, e)]

    loads[10].wait()
    weighted[...] = jnp.zeros_like(weighted)
    norm_scale = 1.0 / (S * math.sqrt(groups * n * ns))
    per = groups // tay

    def peer(d):
        return lax.rem(group + d, groups)

    def gain_of(e):
        if e == 0:
            return gain
        if e > 1:
            beam_copy(e).wait_recv()
        far = beams[e].astype(F32)
        return jnp.concatenate([far[:rows], far[rows:]], axis=1)

    for s in range(ns):

        def collect(e, carry):
            for u, j in enumerate(blocks):
                if u > 0:
                    back_copy(s, e, u, j, owner(me, e), j).wait_recv()
            lhs = jnp.concatenate([back[s, e, j] for j in blocks], axis=0)
            for q in range(qs):
                z = jnp.dot(lhs, t_bwd[q], preferred_element_type=F32)
                cut = slice(q * lanes, (q + 1) * lanes)
                acc = weighted[e, :, cut]
                for u, j in enumerate(blocks):
                    for c in range(2):
                        ramp = ramps[j, s, c, q : q + 1, :]
                        part = z[u * rt : (u + 1) * rt, c * lanes : (c + 1) * lanes]
                        acc = acc + part * ramp
                weighted[e, :, cut] = acc
            return carry

        for r in (1, 0):
            acted = range(1, sets) if r else range(1)
            lax.fori_loop(acted.start, acted.stop, collect, 0)
            if s < ns - 1:
                continue
            for e in acted:
                scaled = gain_of(e) * norm_scale
                for f in range(groups):
                    t = f // per
                    for q in range(width // lanes):
                        at = (f % per) * width + q * lanes
                        cut = slice(at, at + lanes)
                        top = e * tall + q * rows
                        stage_f32[f, top : top + rows, :] = (
                            weighted[e, t * rows : (t + 1) * rows, cut] * scaled[:, cut]
                        )
            low, high = acted.start * tall, acted.stop * tall
            image[:, low:high, :] = stage_f32[:, low:high, :].astype(BF)

            def share(d, carry):
                sum_copy(r, peer(d), group).start()
                return carry

            lax.fori_loop(1, groups, share, 0)

    for r in (1, 0):
        acted = range(1, sets) if r else range(1)
        low, high = acted.start * tall, acted.stop * tall

        def add(d, running):
            j = peer(d)
            sum_copy(r, j, j).wait_recv()
            return running + parts[j, low:high, :].astype(F32)

        summed = lax.fori_loop(1, groups, add, stage_f32[group, low:high, :])
        for e in acted:
            total[e] = summed[e * tall - low : (e + 1) * tall - low]
            if e > 1:
                home_copy(e).start()
        if r == 1:
            home_copy(2).wait_recv()
            total[1] += homes[2]
            home_copy(1).start()
    whole = total[0]
    for e in (3, 1):
        home_copy(e).wait_recv()
        whole = whole + homes[e]
    pieces = [whole[q * rows : (q + 1) * rows] for q in range(width // lanes)]
    result[...] = jnp.concatenate(pieces, axis=1)

    def publish(d, carry):
        out_copy(peer(d), group).start()
        return carry

    lax.fori_loop(1, groups, publish, 0)
    dirty_ref[:, pl.ds(pl.multiple_of(group * width, lanes), width)] = result[...]

    for e in range(1, sets):
        for part in range(2):
            pair_copy(e, part).wait_send()
        beam_copy(e).wait_send()
        home_copy(e).wait_send()

    def finish(k, carry):
        to = other(k)
        of = actor(k)
        fact_copy(k, of, me).wait_send()
        for s in range(ns):
            for e in range(sets):
                msg_copy(s, e, k, to, me).wait_send()
        return carry

    lax.fori_loop(1, close, finish, 0)

    def finish_back(k, carry):
        of = actor(k)
        for s in range(ns):
            for e in range(sets):
                back_copy(s, e, k, of, owner(of, e), me).wait_send()
        return carry

    lax.fori_loop(1, close, finish_back, 0)

    def close(d, carry):
        j = peer(d)
        for r in range(2):
            sum_copy(r, j, group).wait_send()
        out_copy(j, group).wait_send()
        out_copy(j, j).wait_recv()
        return carry

    lax.fori_loop(1, groups, close, 0)


def shards(model, beam, vis_obs, vis_uv, spectral, vis_subgrid, counts, uv_offsets, w_planes):
    rows = model.shape[0]
    fs = beam.shape[-1]
    tay = model.shape[1] // fs
    n = lax.axis_size("vis")
    groups = lax.axis_size("freq")
    extent = rows * n
    ns = w_planes.shape[-1]
    nv = vis_obs.shape[-1]
    rt = tay * rows
    wide = 2 * S
    lanes = 128
    qs = fs // lanes

    t_re, t_im = dft_tables(fs)
    fwd = np.concatenate(
        [np.concatenate([t_re.T, t_im.T], 1), np.concatenate([-t_im.T, t_re.T], 1)], 0
    )
    split = (S, qs, 1, lanes)
    re, im = t_re.reshape(split), t_im.reshape(split)
    bwd = np.concatenate(
        [np.concatenate([re, -im], 2), np.concatenate([im, re], 2)], 0
    )
    bwd = bwd.reshape(2 * S, qs, 2 * lanes).transpose(1, 0, 2)

    tall = rows * tay * fs // groups // lanes
    dma = pltpu.SemaphoreType.DMA
    vmem = pl.BlockSpec(memory_space=pltpu.VMEM)
    hbm = pl.BlockSpec(memory_space=pltpu.HBM)
    dims = (n, groups, tay, rows, fs, ns, nv)
    return pl.pallas_call(
        functools.partial(whole_kernel, dims),
        name="whole",
        out_shape=(
            jax.ShapeDtypeStruct((1, 1, 2, nv), F32),
            jax.ShapeDtypeStruct((rows, tay * fs), F32),
        ),
        in_specs=[hbm] * 11,
        out_specs=(vmem, vmem),
        scratch_shapes=[
            pltpu.VMEM((rows, tay * fs), BF),
            pltpu.VMEM((1, rows, fs), BF),
            pltpu.VMEM((1, 1, 2, nv), F32),
            pltpu.VMEM((1, 1, 2, nv), F32),
            pltpu.VMEM((1, 1, nv), F32),
            pltpu.VMEM((1, 1, nv), I32),
            pltpu.SMEM((1, 1), I32),
            pltpu.SMEM((1, 1, 2, ns), I32),
            pltpu.SMEM((1, 1, ns), I32),
            pltpu.VMEM((2 * fs, wide), BF),
            pltpu.VMEM((qs, wide, 2 * lanes), BF),
            pltpu.VMEM((1, lanes), F32),
            pltpu.VMEM((n, 1, lanes), F32),
            pltpu.VMEM((n, ns, 2, qs, lanes), F32),
            pltpu.VMEM((4, rt, fs), BF),
            pltpu.VMEM((4, 2 * rows, fs // 2), BF),
            pltpu.VMEM((4, rt, fs), F32),
            pltpu.VMEM((8 * rt, 2 * fs), BF),
            pltpu.VMEM((ns, 4, n, rt, wide), BF),
            pltpu.VMEM((ns, n, rt, wide), BF),
            pltpu.VMEM((tay, extent, wide), BF),
            pltpu.VMEM((ns, wide, extent), BF),
            pltpu.VMEM((ns, extent, wide), BF),
            pltpu.VMEM((S, nv), F32),
            pltpu.VMEM((ns, wide, nv), BF),
            pltpu.VMEM((2 * tay * S, wide), BF),
            pltpu.VMEM((2 * tay * S, wide), F32),
            pltpu.VMEM((tay, extent, wide), F32),
            pltpu.VMEM((ns, n, rt, wide), BF),
            pltpu.VMEM((ns, 4, n, rt, wide), BF),
            pltpu.VMEM((groups, 4 * tall, lanes), BF),
            pltpu.VMEM((groups, 4 * tall, lanes), BF),
            pltpu.VMEM((groups, 4 * tall, lanes), F32),
            pltpu.VMEM((4, tall, lanes), F32),
            pltpu.VMEM((4, tall, lanes), F32),
            pltpu.VMEM((rows, tay * fs // groups), F32),
            dma((11,)),
            dma((n // 4,)), dma((n // 4,)),
            dma((8,)), dma((8,)),
            dma((4,)), dma((4,)),
            dma((4,)), dma((4,)),
            dma((ns, 4, n // 4)), dma((ns, 4, n // 4)),
            dma((ns, 4, n // 4)), dma((ns, 4, n // 4)),
            dma((2, groups)), dma((2, groups)),
            dma((groups,)), dma((groups,)),
        ],
        compiler_params=pltpu.CompilerParams(
            collective_id=0, has_side_effects=True, vmem_limit_bytes=60 * 2**20
        ),
    )(
        model, beam, vis_obs, vis_uv, spectral, vis_subgrid, counts, uv_offsets, w_planes,
        np.ascontiguousarray(fwd).astype(BF), np.ascontiguousarray(bwd).astype(BF),
    )


def solution(mesh):
    in_specs = (
        P("vis", None),
        P("freq", "vis", None),
        P("freq", "vis", None, None),
        P("freq", "vis", None, None),
        P("freq", "vis", None),
        P("freq", "vis", None),
        P("freq", "vis"),
        P("freq", "vis", None, None),
        P("freq", "vis", None),
    )
    out_specs = (P("freq", "vis", None, None), P("vis", None))
    return jax.shard_map(shards, mesh=mesh, in_specs=in_specs, out_specs=out_specs, check_vma=False)
```

time: 83.7 us -> 81.8 us (0.977)
  Pallas kernels: 79.3 us -> 77.4 us
    pallas_call x1, Pallas kernels: 79.3 us -> 77.4 us  [shards(): pl.pallas_call(functools.partial(whole_kernel, dims), name='whole', out_s...]
where the time goes in v4:
time: 81.8 us; the launch traced here: 81.6 us
  Pallas kernels  77.4 us (95%)
  local copies, waits for them, and re-layouts  2.89 us (4%)
  between operations  1.29 us (2%)
    pallas_call x1, Pallas kernels, shards(): pl.pallas_call(functools.partial(whole_kernel, dims), name='whole', out_s...  77.4 us
    unnamed x2, local copies, waits for them, and re-layouts  2.89 us

profile of v4, /device:TPU:1, one launch (start us, length us, event | category | flops | bytes accessed | tf_op | source)
XLA Modules:
  0.0 81.6 jit_solution(5866626592549815907)
XLA Ops:
  1.3 77.4 %whole.1 = (f32[1,1,2,2048]{3,2,1,0:T(2,128)}, f32[8,4096]{1,0:T(8,128)}) custom-call(bf16[8,4096]{1,0:T(8,128)(2,1)} %model_hbm.1, bf16[1,8,1024]{2,1,0:T(8,128)(2,1)} %beam_hbm.1, f32[1,1,2,2048]{3,2,1,0:T(2,128)} %obs_hbm.1, f32[1,1,2,2048]{3,2,1,0:T(2,128)} %uv_hbm.1, f32[1,1,2048]{2,1,0:T(1,128)} %spec_hbm.1, s32[1,1,2048]{2,1,0:T(1,128)} %sub_hbm.1, ...), custom_call_target="tpu_custom_call" | custom-call | tf_op jit(solution)/shard_map/whole/pallas_call | solution.py:543
  78.7 1.3 %copy.16 = f32[1,1,2,2048]{3,2,1,0:T(2,128)} copy(f32[1,1,2,2048]{3,2,1,0:T(2,128)} %get-tuple-element.4) | data formatting | bytes 32768
  80.0 1.6 %copy.17 = f32[8,4096]{1,0:T(8,128)} copy(f32[8,4096]{1,0:T(8,128)} %get-tuple-element.5) | data formatting | bytes 262144

commit v5 on v4

--- a/solution.py
+++ b/solution.py
@@ -52,8 +52,8 @@
     dims,
     model_hbm, beam_hbm, obs_hbm, uv_hbm, spec_hbm, sub_hbm, counts_hbm, off_hbm, w_hbm,
     fwd_hbm, bwd_hbm,
-    res_ref, dirty_ref,
-    model_ref, beam_ref, obs_ref, uv_ref, spec_ref, sub_ref, counts_ref, off_ref, w_ref,
+    res_hbm, dirty_hbm,
+    res_ref, model_ref, beam_ref, obs_ref, uv_ref, spec_ref, sub_ref, counts_ref, off_ref, w_ref,
     t_fwd, t_bwd, mine, facts, ramps, hold, beams, weighted,
     xbuf, sends, got, stage, eu, eu_t, ku, kv, grid, gridded, h, back_sends, back, image, parts,
     stage_f32, total, homes, result,
@@ -97,9 +97,10 @@
 
     def pair_copy(e, part):
         cut = pl.ds(part * (rt // 2), rt // 2)
+        way = e if e != 2 else (1, 3)[part]
         return remote(
-            hold.at[1 if e == 2 else 0, cut], hold.at[e, cut],
-            pair_s.at[2 * e + part], pair_r.at[2 * e + part], "vis", helper(1 if e == 2 else e),
+            hold.at[way if e == 2 else 0, cut], hold.at[e, cut],
+            pair_s.at[2 * e + part], pair_r.at[2 * e + part], "vis", helper(way),
         )
 
     def beam_copy(e):
@@ -137,7 +138,7 @@
     width = tay * fs // groups
 
     def out_copy(to, slot):
-        place = dirty_ref.at[:, pl.ds(pl.multiple_of(slot * width, lanes), width)]
+        place = dirty_hbm.at[:, pl.ds(pl.multiple_of(slot * width, lanes), width)]
         return remote(result, place, out_s.at[to], out_r.at[slot], "freq", to)
 
     loads = [
@@ -192,9 +193,8 @@
     beams[0] = jnp.concatenate([gain[:, : fs // 2], gain[:, fs // 2 :]], axis=0).astype(BF)
 
     pl.semaphore_wait(barrier, close + 2 + groups - 1)
-    for e in (1, 3):
-        for part in range(2):
-            pair_copy(e, part).start()
+    for e, part in ((1, 0), (3, 1), (1, 1), (3, 0)):
+        pair_copy(e, part).start()
 
     def tell(k, carry):
         fact_copy(k, actor(k), me).start()
@@ -281,12 +281,12 @@
 
     lax.fori_loop(0, nv // step, kernels, 0)
 
-    for part in range(2):
-        pair_copy(1, part).wait_recv()
+    for part, e in ((0, 1), (1, 3)):
+        pair_copy(e, part).wait_recv()
         pair_copy(2, part).start()
     for e in (1, 3, 2):
-        if e > 1:
-            for part in range(2):
+        for part in range(2):
+            if (e, part) not in ((1, 0), (3, 1)):
                 pair_copy(e, part).wait_recv()
         weighted[e] = hold[e].astype(F32)
         lax.fori_loop(0, ns, functools.partial(forward, e), 0)
@@ -381,6 +381,9 @@
         for e in range(sets):
             back[s, e, me] = back_sends[s, owner(me, e)]
 
+    res_copy = pltpu.make_async_copy(res_ref, res_hbm, tab_sem.at[11])
+    res_copy.start()
+
     loads[10].wait()
     weighted[...] = jnp.zeros_like(weighted)
     norm_scale = 1.0 / (S * math.sqrt(groups * n * ns))
@@ -471,7 +474,9 @@
         return carry
 
     lax.fori_loop(1, groups, publish, 0)
-    dirty_ref[:, pl.ds(pl.multiple_of(group * width, lanes), width)] = result[...]
+    place = dirty_hbm.at[:, pl.ds(pl.multiple_of(group * width, lanes), width)]
+    own_copy = pltpu.make_async_copy(result, place, tab_sem.at[12])
+    own_copy.start()
 
     for e in range(1, sets):
         for part in range(2):
@@ -508,6 +513,8 @@
         return carry
 
     lax.fori_loop(1, groups, close, 0)
+    own_copy.wait()
+    res_copy.wait()
 
 
 def shards(model, beam, vis_obs, vis_uv, spectral, vis_subgrid, counts, uv_offsets, w_planes):
@@ -537,7 +544,6 @@
 
     tall = rows * tay * fs // groups // lanes
     dma = pltpu.SemaphoreType.DMA
-    vmem = pl.BlockSpec(memory_space=pltpu.VMEM)
     hbm = pl.BlockSpec(memory_space=pltpu.HBM)
     dims = (n, groups, tay, rows, fs, ns, nv)
     return pl.pallas_call(
@@ -548,8 +554,9 @@
             jax.ShapeDtypeStruct((rows, tay * fs), F32),
         ),
         in_specs=[hbm] * 11,
-        out_specs=(vmem, vmem),
+        out_specs=(hbm, hbm),
         scratch_shapes=[
+            pltpu.VMEM((1, 1, 2, nv), F32),
             pltpu.VMEM((rows, tay * fs), BF),
             pltpu.VMEM((1, rows, fs), BF),
             pltpu.VMEM((1, 1, 2, nv), F32),
@@ -586,7 +593,7 @@
             pltpu.VMEM((4, tall, lanes), F32),
             pltpu.VMEM((4, tall, lanes), F32),
             pltpu.VMEM((rows, tay * fs // groups), F32),
-            dma((11,)),
+            dma((13,)),
             dma((n // 4,)), dma((n // 4,)),
             dma((8,)), dma((8,)),
             dma((4,)), dma((4,)),

time: 81.8 us -> 78.5 us (0.960)
  Pallas kernels: 77.4 us -> 74.1 us
    pallas_call x1, Pallas kernels: 77.4 us -> 74.1 us  [shards(): pl.pallas_call(functools.partial(whole_kernel, dims), name='whole', out_s...]
where the time goes in v5:
time: 78.5 us; the launch traced here: 78.3 us
  Pallas kernels  74.1 us (94%)
  local copies, waits for them, and re-layouts  2.89 us (4%)
  between operations  1.29 us (2%)
    pallas_call x1, Pallas kernels, shards(): pl.pallas_call(functools.partial(whole_kernel, dims), name='whole', out_s...  74.1 us
    unnamed x2, local copies, waits for them, and re-layouts  2.89 us

profile of v5, /device:TPU:1, one launch (start us, length us, event | category | flops | bytes accessed | tf_op | source)
XLA Modules:
  0.0 78.3 jit_solution(11634669121781242824)
XLA Ops:
  1.3 74.1 %whole.1 = (f32[1,1,2,2048]{3,2,1,0:T(2,128)}, f32[8,4096]{1,0:T(8,128)}) custom-call(bf16[8,4096]{1,0:T(8,128)(2,1)} %model_hbm.1, bf16[1,8,1024]{2,1,0:T(8,128)(2,1)} %beam_hbm.1, f32[1,1,2,2048]{3,2,1,0:T(2,128)} %obs_hbm.1, f32[1,1,2,2048]{3,2,1,0:T(2,128)} %uv_hbm.1, f32[1,1,2048]{2,1,0:T(1,128)} %spec_hbm.1, s32[1,1,2048]{2,1,0:T(1,128)} %sub_hbm.1, ...), custom_call_target="tpu_custom_call" | custom-call | tf_op jit(solution)/shard_map/whole/pallas_call | solution.py:549
  75.4 1.3 %copy.16 = f32[1,1,2,2048]{3,2,1,0:T(2,128)} copy(f32[1,1,2,2048]{3,2,1,0:T(2,128)} %get-tuple-element.4) | data formatting | bytes 32768
  76.7 1.6 %copy.17 = f32[8,4096]{1,0:T(8,128)} copy(f32[8,4096]{1,0:T(8,128)} %get-tuple-element.5) | data formatting | bytes 262144
